TPU v7x, 512 devices: a whole 4x8x8 slice. The times are simulated.
512 devices in a mesh: row: 32 (over x_lo, z, core), col: 16 (over x_hi, y).
Axes of the slice: x: 4 (x_hi: 2, x_lo: 2; x = x_hi * 2 + x_lo), y: 8, z: 8, core: 2. Of those that a mesh axis runs over, the one named last changes fastest.
Arguments:
- users: float32 [32768, 256], P(('row', 'col')), may hold values from -6 to 6
- items: float32 [32768, 256], P(('col', 'row')), may hold values from -0.75 to 0.75
- tiles: bfloat16 [32, 16, 4, 256, 256], P('row', 'col'), may hold values from -0.03125 to 0.03125
- tile_pos: int32 [32, 16, 4], P('row', 'col'), may hold values from 0 to 31, as said below
- tile_count: int32 [32, 16], P('row', 'col'), may hold values from 1 to 4, as said below
- user_ids: int32 [131072], P(('row', 'col')), may hold values from 0 to 32767, as said below
- pos_ids: int32 [131072], P(('row', 'col')), may hold values from 0 to 32767, as said below
- neg_ids: int32 [131072], P(('row', 'col')), may hold values from 0 to 32767, as said below
Outputs:
- grad_users: float32 [32768, 256], P(('row', 'col'))
- grad_items: float32 [32768, 256], P(('col', 'row'))
Inputs may be any that keep to these rules, and one draw needn't show every extreme that they name: `tile_count`: every cell has between 1 and 4 live slots, and some cell has all 4 live. `tile_pos`: the 4 positions of one cell are distinct numbers of 0 to 31; only the live ones count. `user_ids`: the triplets of the device at mesh index (r, c) name only that device's users, rows (r * 16 + c) * 64 to (r * 16 + c + 1) * 64 - 1. `pos_ids`: the triplets of the device at mesh index (r, c) name only that device's items, rows (c * 32 + r) * 64 to (c * 32 + r + 1) * 64 - 1. `neg_ids`: like pos_ids, and never equal to the same triplet's positive item.
All inputs are finite; a program needn't handle non-finite values.
Results may differ from a plain program's by a relative error of at most 0.003.
Values may be sent and summed in bfloat16 or wider, within the bound.
A program may use at most 64 MiB of HBM per device.

v0:
```python
import jax
import jax.numpy as jnp
from jax import lax
from jax.sharding import PartitionSpec as P


def reduce_users(partial_value, usr_dev):
    summed = lax.psum(partial_value, "col")
    return lax.dynamic_slice_in_dim(summed, lax.axis_index("col") * usr_dev, usr_dev, 0)


def reduce_items(partial_value, itm_dev):
    summed = lax.psum(partial_value, "row")
    return lax.dynamic_slice_in_dim(summed, lax.axis_index("row") * itm_dev, itm_dev, 0)


def spread(user_side, item_side, tile_blocks, places, filled):
    usr_dev, embed_width = user_side.shape
    itm_dev = item_side.shape[0]
    tile_size = tile_blocks.shape[1]
    user_count = usr_dev * lax.axis_size("col") // tile_size
    item_count = itm_dev * lax.axis_size("row") // tile_size
    user_panel = lax.all_gather(user_side, "col", axis=0, tiled=True).reshape(
        user_count, tile_size, embed_width
    )
    item_panel = lax.all_gather(item_side, "row", axis=0, tiled=True).reshape(
        item_count, tile_size, embed_width
    )
    user_start = jnp.zeros((user_count, tile_size, embed_width), jnp.float32)
    item_start = jnp.zeros((item_count, tile_size, embed_width), jnp.float32)

    def into_users(slot_index, to_users):
        placed = places[slot_index]
        weights = tile_blocks[slot_index]
        item_rows = item_panel[placed % item_count]
        return to_users.at[placed // item_count].add(
            jnp.dot(weights, item_rows, preferred_element_type=jnp.float32)
        )

    def into_items(slot_index, to_items):
        placed = places[slot_index]
        weights = tile_blocks[slot_index]
        user_rows = user_panel[placed // item_count]
        product = lax.dot_general(
            weights, user_rows, (((0,), (0,)), ((), ())), preferred_element_type=jnp.float32
        )
        return to_items.at[placed % item_count].add(product)

    def both_ways(slot_index, carry):
        return (into_users(slot_index, carry[0]), into_items(slot_index, carry[1]))

    to_users, to_items = lax.fori_loop(0, filled, both_ways, (user_start, item_start))
    user_total = reduce_users(to_users.reshape(user_count * tile_size, embed_width), usr_dev)
    item_total = reduce_items(to_items.reshape(item_count * tile_size, embed_width), itm_dev)
    return (user_total, item_total)


def on_device(users, items, tiles, tile_pos, tile_count, user_ids, pos_ids, neg_ids):
    usr_dev = users.shape[0]
    itm_dev = items.shape[0]
    tile_blocks = tiles[0, 0]
    places = tile_pos[0, 0]
    filled = tile_count[0, 0]
    first_users, first_items = spread(
        users.astype(jnp.bfloat16), items.astype(jnp.bfloat16), tile_blocks, places, filled
    )
    final_users = 0.5 * (users + first_users)
    final_items = 0.5 * (items + first_items)
    user_base = (lax.axis_index("row") * lax.axis_size("col") + lax.axis_index("col")) * usr_dev
    item_base = (lax.axis_index("col") * lax.axis_size("row") + lax.axis_index("row")) * itm_dev
    local_users = user_ids - user_base
    local_pos = pos_ids - item_base
    local_neg = neg_ids - item_base
    chosen = final_users[local_users]
    contrast = final_items[local_pos] - final_items[local_neg]
    score = jnp.sum(chosen * contrast, axis=1)
    back = jax.nn.sigmoid(-score)[:, None]
    user_hot = (local_users[:, None] == jnp.arange(usr_dev, dtype=jnp.int32)[None, :]).astype(
        jnp.float32
    )
    item_hot = (local_neg[:, None] == jnp.arange(itm_dev, dtype=jnp.int32)[None, :]).astype(
        jnp.float32
    )
    item_hot = item_hot - (
        local_pos[:, None] == jnp.arange(itm_dev, dtype=jnp.int32)[None, :]
    ).astype(jnp.float32)
    contract_rows = (((0,), (0,)), ((), ()))
    grad_final_users = lax.dot_general(
        user_hot,
        -back * contrast,
        contract_rows,
        precision=lax.Precision.HIGHEST,
        preferred_element_type=jnp.float32,
    )
    grad_final_items = lax.dot_general(
        item_hot,
        back * chosen,
        contract_rows,
        precision=lax.Precision.HIGHEST,
        preferred_element_type=jnp.float32,
    )
    back_users, back_items = spread(
        grad_final_users.astype(jnp.bfloat16),
        grad_final_items.astype(jnp.bfloat16),
        tile_blocks,
        places,
        filled,
    )
    return (0.5 * grad_final_users + 0.5 * back_users, 0.5 * grad_final_items + 0.5 * back_items)


def solution(mesh):
    placed = (
        P(("row", "col"), None),
        P(("col", "row"), None),
        P("row", "col", None, None, None),
        P("row", "col", None),
        P("row", "col"),
        P(("row", "col")),
        P(("row", "col")),
        P(("row", "col")),
    )
    return jax.shard_map(
        on_device,
        mesh=mesh,
        in_specs=placed,
        out_specs=(P(("row", "col"), None), P(("col", "row"), None)),
        check_vma=False,
    )
```

profile of v0, /device:TPU:1, one launch (start us, length us, event | category | flops | bytes accessed | tf_op | source)
XLA Modules:
  0.0 1025.2 jit_solution(16762847236989567404)
XLA Ops:
  7.2 0.0 all-gather.3.cloned.1.call-start
  7.3 1.5 convert_element_type.19
  8.8 0.0 all-gather.3.cloned.1.call-update
  8.8 0.0 all-reduce.5.cloned.1.call-start
  8.8 0.8 convert_element_type.20
  9.7 37.8 %all_gather.13 = bf16[1024,256]{1,0:T(8,128)(2,1)S(1)} all-gather(bf16[64,256]{1,0:T(8,128)(2,1)S(1)} %convert_element_type.20), channel_id=1, replica_groups=mesh['row'=32,'col'=16] {'col'}, dimensions={0}, use_global_device_ids=true | all-gather | bytes 557056 | tf_op jit(solution)/shard_map/all_gather | solution.py:23
  47.5 35.9 %all-gather.3.cloned.1.call-done = bf16[2048,256]{1,0:T(8,128)(2,1)} async-done(((bf16[64,256]{1,0:T(8,128)(2,1)}), bf16[2048,256]{1,0:T(8,128)(2,1)}) %all-gather.3.cloned.1.call-update) | async-done | bytes 1048592 | tf_op jit(solution)/shard_map/all_gather | solution.py:26
  83.4 1.1 broadcast.122.clone
  84.5 0.2 broadcast.123.clone
  84.7 8.7 while.32
  85.4 0.6 dynamic_slice.118
  88.6 0.8 and_reduce_fusion.6
  89.4 2.6 fusion.63
  92.0 0.8 fusion.64
  93.5 0.0 all-reduce.5.cloned.1.call-update
  93.5 0.0 all-reduce.7.cloned.1.call-start
  93.6 1.2 copy-done.1
  94.8 0.0 all-reduce.7.cloned.1.call-update
  94.8 0.0 all-gather.5.cloned.1.call-start
  95.0 174.9 %all-reduce.5.cloned.1.call-done = f32[1024,256]{1,0:T(8,128)} async-done(((f32[1024,256]{1,0:T(8,128)}), f32[1024,256]{1,0:T(8,128)}) %all-reduce.5.cloned.1.call-update) | async-done | bytes 1048592 | tf_op jit(solution)/shard_map/psum | solution.py:8
  269.8 0.8 add_multiply_fusion.3
  270.7 1.0 gather_fusion
  271.7 243.7 %all-reduce.7.cloned.1.call-done = f32[2048,256]{1,0:T(8,128)} async-done(((f32[2048,256]{1,0:T(8,128)}), f32[2048,256]{1,0:T(8,128)}) %all-reduce.7.cloned.1.call-update) | async-done | bytes 2097168 | tf_op jit(solution)/shard_map/psum | solution.py:13
  515.4 0.8 add_multiply_fusion.2
  516.2 1.0 gather_fusion.1
  517.2 1.0 gather_fusion.2
  518.2 0.1 multiply_reduce_fusion
  518.3 1.2 fusion.45
  519.4 0.0 all-gather.5.cloned.1.call-update
  519.5 0.0 all-reduce.9.cloned.1.call-start
  519.5 0.4 fusion.46
  519.9 36.6 %all_gather.15 = bf16[1024,256]{1,0:T(8,128)(2,1)S(1)} all-gather(bf16[64,256]{1,0:T(8,128)(2,1)S(1)} %get-tuple-element.318), channel_id=1, replica_groups=mesh['row'=32,'col'=16] {'col'}, dimensions={0}, use_global_device_ids=true | all-gather | bytes 557056 | tf_op jit(solution)/shard_map/all_gather | solution.py:23
  556.5 28.5 %all-gather.5.cloned.1.call-done = bf16[2048,256]{1,0:T(8,128)(2,1)} async-done(((bf16[64,256]{1,0:T(8,128)(2,1)}), bf16[2048,256]{1,0:T(8,128)(2,1)}) %all-gather.5.cloned.1.call-update) | async-done | bytes 1048592 | tf_op jit(solution)/shard_map/all_gather | solution.py:26
  584.9 1.1 broadcast.122
  586.0 0.2 broadcast.123
  586.2 8.7 while.33
  586.9 0.6 dynamic_slice.123
  590.1 0.8 and_reduce_fusion.7
  590.9 2.6 fusion.69
  593.5 0.8 fusion.70
  594.9 0.0 all-reduce.9.cloned.1.call-update
  595.0 0.0 all-reduce.11.cloned.1.call-start
  595.0 1.2 copy-done
  596.3 0.0 all-reduce.11.cloned.1.call-update
  596.3 175.1 %all-reduce.9.cloned.1.call-done = f32[1024,256]{1,0:T(8,128)} async-done(((f32[1024,256]{1,0:T(8,128)}), f32[1024,256]{1,0:T(8,128)}) %all-reduce.9.cloned.1.call-update) | async-done | bytes 1048592 | tf_op jit(solution)/shard_map/psum | solution.py:8
  771.4 1.5 add_multiply_fusion.1
  772.9 243.9 %all-reduce.11.cloned.1.call-done = f32[2048,256]{1,0:T(8,128)} async-done(((f32[2048,256]{1,0:T(8,128)}), f32[2048,256]{1,0:T(8,128)}) %all-reduce.11.cloned.1.call-update) | async-done | bytes 2097168 | tf_op jit(solution)/shard_map/psum | solution.py:13
  1016.8 1.5 add_multiply_fusion
  (26 shorter events, 0.1 us)
Async XLA Ops:
  7.2 77.5 %copy-start.5 = (s32[3]{0:T(128)S(1)}, s32[3]{0:T(128)}, u32[]{:S(2)}) copy-start(s32[3]{0:T(128)} %constant.239.clone.1) | copy-start | bytes 40
  7.2 77.5 %copy-start.6 = (s32[3]{0:T(128)S(1)}, s32[3]{0:T(128)}, u32[]{:S(2)}) copy-start(s32[3]{0:T(128)} %constant.236.clone.1) | copy-start | bytes 40
  7.2 77.5 %copy-start.10 = (s32[1,1,4]{2,1,0:T(1,128)S(1)}, s32[1,1,4]{2,1,0:T(1,128)}, u32[]{:S(2)}) copy-start(s32[1,1,4]{2,1,0:T(1,128)} %param.23) | copy-start | bytes 52
  7.2 77.5 %copy-start.2 = (bf16[1,1,4,256,256]{4,3,2,1,0:T(8,128)(2,1)S(1)}, bf16[1,1,4,256,256]{4,3,2,1,0:T(8,128)(2,1)}, u32[]{:S(2)}) copy-start(bf16[1,1,4,256,256]{4,3,2,1,0:T(8,128)(2,1)} %param.22) | copy-start | bytes 1572868
  7.2 76.2 %all-gather.3.cloned.1.call-start = ((), (), s32[]{:S(2)}) async-start(), calls=%async_computation | async-start | bytes 1081344 | tf_op jit(solution)/shard_map/all_gather | solution.py:26
  8.8 261.0 %all-reduce.5.cloned.1.call-start = ((), (), s32[]{:S(2)}) async-start(), calls=%async_computation.1 | async-start | bytes 2097152 | tf_op jit(solution)/shard_map/psum | solution.py:8
  93.5 1.3 copy-start.1
  93.5 1.4 copy-start.7
  93.5 1.4 copy-start.8
  93.5 1.4 copy-start.9
  93.5 176.3 %copy-start.3 = (f32[64,256]{1,0:T(8,128)S(1)}, f32[64,256]{1,0:T(8,128)}, u32[]{:S(2)}) copy-start(f32[64,256]{1,0:T(8,128)} %param.20) | copy-start | bytes 196612
  93.5 421.8 %all-reduce.7.cloned.1.call-start = ((), (), s32[]{:S(2)}) async-start(), calls=%async_computation.2 | async-start | bytes 4194304 | tf_op jit(solution)/shard_map/psum | solution.py:13
  93.6 421.8 %copy-start.4 = (f32[64,256]{1,0:T(8,128)S(1)}, f32[64,256]{1,0:T(8,128)}, u32[]{:S(2)}) copy-start(f32[64,256]{1,0:T(8,128)} %param.21) | copy-start | bytes 196612
  94.8 490.1 %all-gather.5.cloned.1.call-start = ((), (), s32[]{:S(2)}) async-start(), calls=%async_computation.3 | async-start | bytes 1081344 | tf_op jit(solution)/shard_map/all_gather | solution.py:26
  519.5 252.0 %all-reduce.9.cloned.1.call-start = ((), (), s32[]{:S(2)}) async-start(), calls=%async_computation.4 | async-start | bytes 2097152 | tf_op jit(solution)/shard_map/psum | solution.py:8
  594.9 1.3 copy-start
  595.0 421.9 %all-reduce.11.cloned.1.call-start = ((), (), s32[]{:S(2)}) async-start(), calls=%async_computation.5 | async-start | bytes 4194304 | tf_op jit(solution)/shard_map/psum | solution.py:13
Sparse Core Ops, SparseCore 0:
  10.8 72.6 all-gather.2
  93.7 176.1 all-reduce.4
  273.0 242.2 all-reduce.6
  519.6 65.2 all-gather.4
  595.1 176.2 all-reduce.8
  774.5 242.3 all-reduce.10
where the time goes:
time: 1030 us
  waiting for transfers between devices  902 us (88%)
  blocking collectives  74.4 us (7%)
  between operations  14.4 us (1%)
    psum x2, waiting for transfers between devices, reduce_items(): summed = lax.psum(partial_value, 'row')  488 us
    psum x2, waiting for transfers between devices, reduce_users(): summed = lax.psum(partial_value, 'col')  350 us
    all_gather x2, blocking collectives, spread(): lax.all_gather(user_side, 'col', axis=0, tiled=True)  74.4 us
    all_gather x2, waiting for transfers between devices, spread(): lax.all_gather(item_side, 'row', axis=0, tiled=True)  64.4 us
  transfers between devices with their start and end apart: 6, of which 6 were waited for; matrix products, arithmetic and copies ran while one was open for 0% of the time, Pallas kernels for 0%

commit v1 on v0

v1 whole, which is shorter than its diff:
```python
import functools

import jax
import jax.numpy as jnp
from jax import lax
from jax.experimental import pallas as pl
from jax.experimental.pallas import tpu as pltpu
from jax.sharding import PartitionSpec as P

MESH = pl.DeviceIdType.MESH
BF16 = jnp.bfloat16
F32 = jnp.float32
SLOTS = 4
ROWS = 64
WIDTH = 256
TILE = 256
USER_BLOCKS = 16
ITEM_GROUPS = 16
ITEM_TILES = 8


def masks_of(pos_ref, count_ref):
    filled = count_ref[0, 0]
    masks = []
    for slot in range(SLOTS):
        placed = pos_ref[0, slot]
        live = jnp.full((1, WIDTH), slot, jnp.int32) < jnp.full((1, WIDTH), filled, jnp.int32)
        wide = jnp.full((1, WIDTH), placed, jnp.int32)
        masks.append(
            (placed >> 3, placed & 7, jnp.where(live, wide >> 3, -1), jnp.where(live, wide & 7, -1))
        )
    return masks


def pick(masks, which, index):
    return [jnp.where(mask[2 + which] == index, 1.0, 0.0).astype(F32) for mask in masks]


def kernel(
    users_ref,
    items_ref,
    pos_ref,
    count_ref,
    uid_ref,
    pid_ref,
    nid_ref,
    tiles_hbm,
    out_users_ref,
    out_items_ref,
    tiles,
    tiles_t,
    user_panel_0,
    user_panel_1,
    item_panel_0,
    item_panel_1,
    prod_users,
    prod_items,
    sum_users,
    sum_items,
    mate_items,
    pair_items,
    recv_users,
    recv_items,
    load_sem,
    gu_send,
    gu_recv,
    gi_send,
    gi_recv,
    mi_send,
    mi_recv,
    rm_send,
    rm_recv,
    ru_send,
    ru_recv,
    ri_send,
    ri_recv,
):
    row = lax.axis_index("row")
    col = lax.axis_index("col")
    core = lax.rem(row, 2)
    group = row // 2
    mate = (row + 1 - 2 * core, col)

    def user_peer(step):
        return (row, lax.rem(col + step, USER_BLOCKS))

    def item_peer(step):
        return (lax.rem(group + step, ITEM_GROUPS) * 2 + core, col)

    load = pltpu.make_async_copy(tiles_hbm, tiles, load_sem)
    load.start()

    barrier = pltpu.get_barrier_semaphore()
    for step in range(1, USER_BLOCKS):
        pl.semaphore_signal(barrier, 1, device_id=user_peer(step), device_id_type=MESH)
        pl.semaphore_signal(barrier, 1, device_id=item_peer(step), device_id_type=MESH)
    pl.semaphore_signal(barrier, 1, device_id=mate, device_id_type=MESH)
    pl.semaphore_wait(barrier, 2 * (USER_BLOCKS - 1) + 1)

    masks = masks_of(pos_ref, count_ref)
    user_panel = (user_panel_0, user_panel_1)
    item_panel = (item_panel_0, item_panel_1)

    def block_of(panel, position):
        return panel.at[position // 4, lax.rem(position, 4)]

    def gather_users(turn, own):
        panel = user_panel[turn]
        block_of(panel, col)[...] = own
        for step in range(1, USER_BLOCKS):
            pltpu.make_async_remote_copy(
                src_ref=block_of(panel, col),
                dst_ref=block_of(panel, col),
                send_sem=gu_send.at[turn],
                recv_sem=gu_recv.at[turn],
                device_id=user_peer(step),
                device_id_type=MESH,
            ).start()

    def item_copy(turn, which_row, step, device):
        panel = item_panel[turn]
        return pltpu.make_async_remote_copy(
            src_ref=block_of(panel, which_row),
            dst_ref=block_of(panel, which_row),
            send_sem=gi_send.at[turn],
            recv_sem=gi_recv.at[turn, step],
            device_id=device,
            device_id_type=MESH,
        )

    def mate_copy(turn, which_row):
        panel = item_panel[turn]
        return pltpu.make_async_remote_copy(
            src_ref=block_of(panel, which_row),
            dst_ref=block_of(panel, which_row),
            send_sem=mi_send.at[turn],
            recv_sem=mi_recv.at[turn],
            device_id=mate,
            device_id_type=MESH,
        )

    def gather_items(turn, own):
        panel = item_panel[turn]
        block_of(panel, row)[...] = own
        for step in range(1, ITEM_GROUPS):
            item_copy(turn, row, step, item_peer(step)).start()
        mate_copy(turn, row).start()

    def bulk_wait(ref, send_sem, recv_sem, send):
        copy = pltpu.make_async_remote_copy(
            src_ref=ref, dst_ref=ref, send_sem=send_sem, recv_sem=recv_sem,
            device_id=mate, device_id_type=MESH,
        )
        if send:
            copy.wait_send()
        else:
            copy.wait_recv()

    def relay_items(turn):
        for step in range(1, ITEM_GROUPS):
            source = lax.rem(group + ITEM_GROUPS - step, ITEM_GROUPS) * 2 + core
            item_copy(turn, source, step, mate).wait_recv()
            mate_copy(turn, source).start()
        half = item_panel[turn].at[pl.ds(0, 4)]
        bulk_wait(half, mi_send.at[turn], mi_recv.at[turn], False)

    def spread(turn):
        for slot in range(SLOTS):
            placed = item_panel[turn][masks[slot][1]].reshape(TILE, WIDTH)
            prod_users[slot] = jnp.dot(tiles[slot], placed, preferred_element_type=F32)

        def add_users(block, carry):
            weights = pick(masks, 0, block // 4)
            rows = pl.ds(pl.multiple_of(lax.rem(block, 4) * ROWS, ROWS), ROWS)
            total = weights[0] * prod_users[0, rows, :]
            for slot in range(1, SLOTS):
                total += weights[slot] * prod_users[slot, rows, :]
            sum_users[turn, block] = total.astype(BF16)
            return carry

        lax.fori_loop(0, USER_BLOCKS, add_users, 0)
        for step in range(1, USER_BLOCKS):
            pltpu.make_async_remote_copy(
                src_ref=sum_users.at[turn, lax.rem(col + step, USER_BLOCKS)],
                dst_ref=recv_users.at[turn, step],
                send_sem=ru_send.at[turn],
                recv_sem=ru_recv.at[turn],
                device_id=user_peer(step),
                device_id_type=MESH,
            ).start()

    def spread_items(turn):
        for slot in range(SLOTS):
            placed = user_panel[turn][masks[slot][0]].reshape(TILE, WIDTH)
            prod_items[slot] = jnp.dot(tiles_t[slot], placed, preferred_element_type=F32)

        def add_items(block, carry):
            weights = pick(masks, 1, block // 4)
            rows = pl.ds(pl.multiple_of(lax.rem(block, 4) * ROWS, ROWS), ROWS)
            total = weights[0] * prod_items[0, rows, :]
            for slot in range(1, SLOTS):
                total += weights[slot] * prod_items[slot, rows, :]
            sum_items[turn, lax.rem(block, 2), block // 2] = total.astype(BF16)
            return carry

        lax.fori_loop(0, 2 * ITEM_GROUPS, add_items, 0)
        pltpu.make_async_remote_copy(
            src_ref=sum_items.at[turn, 1 - core],
            dst_ref=mate_items.at[turn],
            send_sem=rm_send.at[turn],
            recv_sem=rm_recv.at[turn],
            device_id=mate,
            device_id_type=MESH,
        ).start()

    def pair_up(turn):
        bulk_wait(mate_items.at[turn], rm_send.at[turn], rm_recv.at[turn], False)

        def add_pair(block, carry):
            pair_items[turn, block] = (
                sum_items[turn, core, block].astype(F32) + mate_items[turn, block].astype(F32)
            ).astype(BF16)
            return carry

        lax.fori_loop(0, ITEM_GROUPS, add_pair, 0)
        for step in range(1, ITEM_GROUPS):
            pltpu.make_async_remote_copy(
                src_ref=pair_items.at[turn, lax.rem(group + step, ITEM_GROUPS)],
                dst_ref=recv_items.at[turn, step],
                send_sem=ri_send.at[turn],
                recv_sem=ri_recv.at[turn],
                device_id=item_peer(step),
                device_id_type=MESH,
            ).start()

    def total_of(own, received):
        total = own.astype(F32)
        for step in range(1, USER_BLOCKS):
            total += received[step].astype(F32)
        return total

    def propagate(turn, own_users, own_items):
        gather_items(turn, own_items)
        gather_users(turn, own_users)
        if turn == 0:
            load.wait()
            for slot in range(SLOTS):
                tiles_t[slot] = tiles[slot].T
        bulk_wait(
            recv_users.at[turn, pl.ds(1, USER_BLOCKS - 1)],
            gu_send.at[turn], gu_recv.at[turn], False,
        )
        spread_items(turn)
        relay_items(turn)
        spread(turn)
        pair_up(turn)
        first = pl.ds(1, USER_BLOCKS - 1)
        bulk_wait(recv_users.at[turn, first], ru_send.at[turn], ru_recv.at[turn], False)
        to_users = total_of(sum_users[turn, col], recv_users.at[turn])
        bulk_wait(recv_items.at[turn, first], ri_send.at[turn], ri_recv.at[turn], False)
        to_items = total_of(pair_items[turn, group], recv_items.at[turn])
        return to_users, to_items

    first_users, first_items = propagate(
        0, users_ref[...].astype(BF16), items_ref[...].astype(BF16)
    )
    final_users = 0.5 * (users_ref[...] + first_users)
    final_items = 0.5 * (items_ref[...] + first_items)

    user_base = (row * USER_BLOCKS + col) * ROWS
    item_base = (col * 2 * ITEM_GROUPS + row) * ROWS
    batch = uid_ref.shape[1]
    places = lax.broadcasted_iota(jnp.int32, (ROWS, batch), 0)
    user_hot = jnp.where(places == uid_ref[...] - user_base, 1.0, 0.0).astype(F32)
    item_hot = jnp.where(places == nid_ref[...] - item_base, 1.0, 0.0).astype(F32)
    item_hot = item_hot - jnp.where(places == pid_ref[...] - item_base, 1.0, 0.0).astype(F32)
    dot = functools.partial(
        jnp.dot, precision=lax.Precision.HIGHEST, preferred_element_type=F32
    )
    chosen = dot(user_hot.T, final_users)
    against = dot(item_hot.T, final_items)
    score = -jnp.sum(chosen * against, axis=1, keepdims=True)
    back = jax.nn.sigmoid(-score)
    grad_users = dot(user_hot, back * against)
    grad_items = dot(item_hot, back * chosen)

    back_users, back_items = propagate(1, grad_users.astype(BF16), grad_items.astype(BF16))
    out_users_ref[...] = 0.5 * grad_users + 0.5 * back_users
    out_items_ref[...] = 0.5 * grad_items + 0.5 * back_items

    for turn in range(2):
        first = pl.ds(1, USER_BLOCKS - 1)
        bulk_wait(recv_users.at[turn, first], gu_send.at[turn], gu_recv.at[turn], True)
        bulk_wait(recv_items.at[turn, first], gi_send.at[turn], gi_recv.at[turn, 0], True)
        half = item_panel[turn].at[pl.ds(0, 4)]
        bulk_wait(half, mi_send.at[turn], mi_recv.at[turn], True)
        bulk_wait(mate_items.at[turn], rm_send.at[turn], rm_recv.at[turn], True)
        bulk_wait(recv_users.at[turn, first], ru_send.at[turn], ru_recv.at[turn], True)
        bulk_wait(recv_items.at[turn, first], ri_send.at[turn], ri_recv.at[turn], True)


def on_device(users, items, tiles, tile_pos, tile_count, user_ids, pos_ids, neg_ids):
    vmem = pl.BlockSpec(memory_space=pltpu.VMEM)
    smem = pl.BlockSpec(memory_space=pltpu.SMEM)
    dma = pltpu.SemaphoreType.DMA
    batch = user_ids.shape[0]
    return pl.pallas_call(
        kernel,
        out_shape=(
            jax.ShapeDtypeStruct((ROWS, WIDTH), F32),
            jax.ShapeDtypeStruct((ROWS, WIDTH), F32),
        ),
        in_specs=[vmem, vmem, smem, smem, vmem, vmem, vmem, pl.BlockSpec(memory_space=pl.ANY)],
        out_specs=(vmem, vmem),
        scratch_shapes=[
            pltpu.VMEM((SLOTS, TILE, TILE), BF16),
            pltpu.VMEM((SLOTS, TILE, TILE), BF16),
            pltpu.VMEM((4, 4, ROWS, WIDTH), BF16),
            pltpu.VMEM((4, 4, ROWS, WIDTH), BF16),
            pltpu.VMEM((ITEM_TILES, 4, ROWS, WIDTH), BF16),
            pltpu.VMEM((ITEM_TILES, 4, ROWS, WIDTH), BF16),
            pltpu.VMEM((SLOTS, TILE, WIDTH), F32),
            pltpu.VMEM((SLOTS, TILE, WIDTH), F32),
            pltpu.VMEM((2, USER_BLOCKS, ROWS, WIDTH), BF16),
            pltpu.VMEM((2, 2, ITEM_GROUPS, ROWS, WIDTH), BF16),
            pltpu.VMEM((2, ITEM_GROUPS, ROWS, WIDTH), BF16),
            pltpu.VMEM((2, ITEM_GROUPS, ROWS, WIDTH), BF16),
            pltpu.VMEM((2, USER_BLOCKS, ROWS, WIDTH), BF16),
            pltpu.VMEM((2, ITEM_GROUPS, ROWS, WIDTH), BF16),
            dma,
            dma((2,)),
            dma((2,)),
            dma((2,)),
            dma((2, ITEM_GROUPS)),
            dma((2,)),
            dma((2,)),
            dma((2,)),
            dma((2,)),
            dma((2,)),
            dma((2,)),
            dma((2,)),
            dma((2,)),
        ],
        compiler_params=pltpu.CompilerParams(
            collective_id=0, has_side_effects=True, vmem_limit_bytes=40 << 20
        ),
        name="propagation_layer",
    )(
        users,
        items,
        tile_pos.reshape(1, SLOTS),
        tile_count,
        user_ids.reshape(1, batch),
        pos_ids.reshape(1, batch),
        neg_ids.reshape(1, batch),
        tiles.reshape(SLOTS, TILE, TILE),
    )


def solution(mesh):
    placed = (
        P(("row", "col"), None),
        P(("col", "row"), None),
        P("row", "col", None, None, None),
        P("row", "col", None),
        P("row", "col"),
        P(("row", "col")),
        P(("row", "col")),
        P(("row", "col")),
    )
    return jax.shard_map(
        on_device,
        mesh=mesh,
        in_specs=placed,
        out_specs=(P(("row", "col"), None), P(("col", "row"), None)),
        check_vma=False,
    )
```

time: 1030 us -> 93.5 us (0.09)
  waiting for transfers between devices: 902 us -> 0 us
  Pallas kernels: 0 us -> 86.9 us
  blocking collectives: 74.4 us -> 0 us
  between operations: 14.4 us -> 1.32 us
    psum x4 -> x0, waiting for transfers between devices: 838 us -> none  [the longest x2 488 us: reduce_items(): summed = lax.psum(partial_value, 'row')]
    pallas_call x0 -> x1, Pallas kernels: none -> 86.9 us  [on_device(): pl.pallas_call(kernel, out_shape=(jax.ShapeDtypeStruct((ROWS, WIDTH), F32...]
    all_gather x2 -> x0, blocking collectives: 74.4 us -> none  [spread(): lax.all_gather(user_side, 'col', axis=0, tiled=True)]
    all_gather x2 -> x0, waiting for transfers between devices: 64.4 us -> none  [spread(): lax.all_gather(item_side, 'row', axis=0, tiled=True)]
  transfers between devices with their start and end apart: 6 -> 0, of which waited for: 6 -> 0; matrix products, arithmetic and copies ran while one was open for 0% -> 0% of each run, Pallas kernels for 0% -> 0%
where the time goes in v1:
time: 93.5 us; the launch traced here: 92.8 us
  Pallas kernels  86.9 us (93%)
  local copies, waits for them, and re-layouts  4.66 us (5%)
  between operations  1.32 us (1%)
    pallas_call x1, Pallas kernels, on_device(): pl.pallas_call(kernel, out_shape=(jax.ShapeDtypeStruct((ROWS, WIDTH), F32...  86.9 us
    unnamed x16, local copies, waits for them, and re-layouts  4.66 us

profile of v1, /device:TPU:1, one launch (start us, length us, event | category | flops | bytes accessed | tf_op | source)
XLA Modules:
  0.0 92.8 jit_solution(1346962296739244710)
XLA Ops:
  1.3 0.0 copy-start.4
  1.3 0.0 copy-start.5
  1.3 0.0 copy-start.3
  1.3 0.0 copy-start.6
  1.3 0.6 copy-done.4
  2.0 0.0 copy-done.5
  2.0 0.0 copy-done.3
  2.0 0.0 copy-done.6
  2.0 0.0 copy-start
  2.0 1.0 %copy-done = bf16[1,1,4,256,256]{4,3,2,1,0:T(8,128)(2,1)S(1)} copy-done((bf16[1,1,4,256,256]{4,3,2,1,0:T(8,128)(2,1)S(1)}, bf16[1,1,4,256,256]{4,3,2,1,0:T(8,128)(2,1)}, u32[]{:S(2)}) %copy-start) | copy-done | bytes 524312
  3.0 0.0 copy-start.1
  3.0 0.8 copy-done.1
  3.9 0.0 copy-start.2
  3.9 0.8 copy-done.2
  4.7 86.9 %propagation_layer.1 = (f32[64,256]{1,0:T(8,128)S(1)}, f32[64,256]{1,0:T(8,128)S(1)}) custom-call(f32[64,256]{1,0:T(8,128)S(1)} %copy-done.1, f32[64,256]{1,0:T(8,128)S(1)} %copy-done.2, s32[1,4]{1,0:T(1,128)S(1)} %bitcast.9, s32[1,1]{1,0:T(1,128)S(6)} %copy.12.count_ref, s32[1,256]{1,0:T(1,128)S(1)} %bitcast.6, s32[1,256]{1,0:T(1,128)S(1)} %bitcast.7, ...), custom_call_target="tpu_custom_call" | custom-call | tf_op jit(solution)/shard_map/propagation_layer/pallas_call | solution.py:307
  91.6 0.6 copy.13
  92.2 0.6 copy.14
Async XLA Ops:
  1.3 0.7 copy-start.4
  1.3 0.7 copy-start.5
  1.3 0.7 copy-start.3
  1.3 0.7 copy-start.6
  2.0 1.0 %copy-start = (bf16[1,1,4,256,256]{4,3,2,1,0:T(8,128)(2,1)S(1)}, bf16[1,1,4,256,256]{4,3,2,1,0:T(8,128)(2,1)}, u32[]{:S(2)}) copy-start(bf16[1,1,4,256,256]{4,3,2,1,0:T(8,128)(2,1)} %param.10) | copy-start | bytes 1572868
  3.0 0.8 copy-start.1
  3.9 0.8 copy-start.2

commit v2 on v0

v2 whole, which is shorter than its diff:
```python
import functools

import jax
import jax.numpy as jnp
from jax import lax
from jax.experimental import pallas as pl
from jax.experimental.pallas import tpu as pltpu
from jax.sharding import PartitionSpec as P

MESH = pl.DeviceIdType.MESH
BF16 = jnp.bfloat16
F32 = jnp.float32
SLOTS = 4
ROWS = 64
HALF = 128
WIDTH = 256
TILE = 256
RING = 8
BLOCKS = 16
USERS, ITEMS = 0, 1


def split(value, parts):
    terms = []
    for part in range(parts):
        term = value.astype(BF16)
        terms.append(term)
        value = value - term.astype(F32)
    return jnp.concatenate(terms, axis=0)


def kernel(
    users_ref,
    items_ref,
    pos_ref,
    count_ref,
    uid_ref,
    pid_ref,
    nid_ref,
    tiles_hbm,
    out_users_ref,
    out_items_ref,
    tiles,
    tiles_t,
    meta,
    meta_smem,
    user_hot,
    item_hot,
    user_hot_t,
    item_hot_t,
    user_panel_0,
    user_panel_1,
    item_panel_0,
    item_panel_1,
    stage,
    prod,
    sums,
    far,
    relayed,
    near,
    x_out,
    x_in,
    pair_sum,
    halves,
    load_sem,
    tile_send,
    tile_recv,
    meta_sem,
    meta_send,
    meta_recv,
    gm_send,
    gm_recv,
    gx_recv,
    g2_recv,
    gb_send,
    gb_recv,
    sf_recv,
    sn_recv,
    s_send,
    sx_send,
    sx_recv,
    sm_send,
    sm_recv,
):
    row = lax.axis_index("row")
    col = lax.axis_index("col")
    core = lax.rem(row, 2)
    group = row // 2
    mate = (row + 1 - 2 * core, col)
    x_at = (col // RING, group // RING)
    ring_at = (lax.rem(col, RING), lax.rem(group, RING))

    def device(which, x, ring):
        if which == USERS:
            return (row, x * RING + ring)
        return ((x * RING + ring) * 2 + core, col)

    def along(which, step):
        return device(which, x_at[which], lax.rem(ring_at[which] + step + RING, RING))

    def across(which):
        return device(which, 1 - x_at[which], ring_at[which])

    def block(which, other, step):
        x = 1 - x_at[which] if other else x_at[which]
        return x * RING + lax.rem(ring_at[which] + step + RING, RING)

    def send(source, target, send_sem, recv_sem, to):
        pltpu.make_async_remote_copy(
            src_ref=source, dst_ref=target, send_sem=send_sem, recv_sem=recv_sem,
            device_id=to, device_id_type=MESH,
        ).start()

    def awaits(ref, sem):
        pltpu.make_async_remote_copy(
            src_ref=ref, dst_ref=ref, send_sem=sem, recv_sem=sem,
            device_id=mate, device_id_type=MESH,
        ).wait_recv()

    def sent(ref, sem):
        pltpu.make_async_remote_copy(
            src_ref=ref, dst_ref=ref, send_sem=sem, recv_sem=sem,
            device_id=mate, device_id_type=MESH,
        ).wait_send()

    barrier = pltpu.get_barrier_semaphore()
    peers = [mate]
    for which in (USERS, ITEMS):
        peers += [across(which)] + [along(which, step) for step in (1, -1, 2, -2)]
    for peer in peers:
        pl.semaphore_signal(barrier, 1, device_id=peer, device_id_type=MESH)

    load = pltpu.make_async_copy(tiles_hbm, tiles.at[core], load_sem)
    load.start()
    filled = jnp.full((8, HALF), count_ref[0, 0], jnp.int32)
    slot_of = lax.broadcasted_iota(jnp.int32, (8, HALF), 0)
    placed = jnp.full((8, HALF), pos_ref[0, 0], jnp.int32)
    for slot in range(1, SLOTS):
        placed = jnp.where(slot_of == slot, jnp.full((8, HALF), pos_ref[0, slot], jnp.int32), placed)
    meta[core] = jnp.where(slot_of < filled, placed, placed + 64)

    panels = ((user_panel_0, item_panel_0), (user_panel_1, item_panel_1))

    def at_block(turn, which, number):
        per = 4 if which == USERS else 2
        return panels[turn][which].at[number // per, lax.rem(number, per)]

    def own_rows(turn, which, value):
        stage[turn, which, 0] = value[:, :HALF].astype(BF16)
        stage[turn, which, 1] = value[:, HALF:].astype(BF16)
        own = at_block(turn, which, block(which, False, 0))
        own[core] = stage[turn, which, core]

    def gather_mate(turn, which):
        own = at_block(turn, which, block(which, False, 0))
        send(stage.at[turn, which, 1 - core], own.at[core],
             gm_send.at[turn, which], gm_recv.at[turn, which], mate)

    def gather_block(turn, which, other):
        here = at_block(turn, which, block(which, other, 0))
        for step in (2, -2):
            send(here, here, gb_send.at[turn, which],
                 g2_recv.at[turn, which, int(other), int(step < 0)], along(which, step))
        for step in (1, -1):
            send(here, here, gb_send.at[turn, which], gb_recv.at[turn, which], along(which, step))

    def gather_own(turn, which):
        own = at_block(turn, which, block(which, False, 0))
        awaits(own.at[1 - core], gm_recv.at[turn, which])
        send(own, own, gb_send.at[turn, which], gx_recv.at[turn, which], across(which))
        gather_block(turn, which, False)

    def gather_across(turn, which):
        awaits(at_block(turn, which, block(which, True, 0)), gx_recv.at[turn, which])
        gather_block(turn, which, True)

    def gather_relay(turn, which, other):
        for way, step in ((0, 1), (1, -1)):
            here = at_block(turn, which, block(which, other, -2 * step))
            awaits(here, g2_recv.at[turn, which, int(other), way])
            part = here.at[way]
            send(part, part, gb_send.at[turn, which], gb_recv.at[turn, which], along(which, 2 * step))
            send(here, here, gb_send.at[turn, which], gb_recv.at[turn, which], along(which, step))

    def gather_end(turn, which):
        awaits(sums.at[turn, which, pl.ds(0, 10)], gb_recv.at[turn, which])

    def marks(cell, slot):
        return meta[cell, pl.ds(slot, 1), :]

    def spread_users(turn):
        panel = panels[turn][ITEMS]
        for cell in range(2):
            for slot in range(SLOTS):
                rows = panel[meta_smem[cell, slot, 0] & 7].reshape(TILE, HALF)
                prod[cell * SLOTS + slot] = jnp.dot(
                    tiles[cell, slot], rows, preferred_element_type=F32
                )

        def add(number, carry):
            start = pl.ds(pl.multiple_of(lax.rem(number, 4) * ROWS, ROWS), ROWS)
            for cell in range(2):
                total = jnp.zeros((ROWS, HALF), F32)
                for slot in range(SLOTS):
                    weight = jnp.where((marks(cell, slot) >> 3) == number // 4, 1.0, 0.0)
                    total += weight.astype(F32) * prod[cell * SLOTS + slot, start, :]
                sums[turn, USERS, number, cell] = total.astype(BF16)
            return carry

        lax.fori_loop(0, BLOCKS, add, 0)

    def spread_items(turn):
        panel = panels[turn][USERS]
        for cell in range(2):
            for slot in range(SLOTS):
                tile = (meta_smem[cell, slot, 0] >> 3) & 3
                rows = panel[tile, :, cell].reshape(TILE, HALF)
                prod[cell * SLOTS + slot] = jnp.dot(
                    tiles_t[cell, slot], rows, preferred_element_type=F32
                )

        def add(number, carry):
            for owner in range(2):
                start = (lax.rem(number, 2) * 2 + owner) * ROWS
                start = pl.ds(pl.multiple_of(start, ROWS), ROWS)
                total = jnp.zeros((ROWS, HALF), F32)
                for cell in range(2):
                    for slot in range(SLOTS):
                        weight = jnp.where((marks(cell, slot) & 71) == number // 2, 1.0, 0.0)
                        total += weight.astype(F32) * prod[cell * SLOTS + slot, start, :]
                sums[turn, ITEMS, number, owner] = total.astype(BF16)
            return carry

        lax.fori_loop(0, BLOCKS, add, 0)

    def scatter_start(turn, which):
        out = s_send.at[turn, which]
        for other in (True, False):
            e = int(other)
            for way, step in ((0, 1), (1, -1)):
                sem = sf_recv.at[turn, which, e, way]
                send(sums.at[turn, which, block(which, other, 4), way],
                     far.at[turn, which, e, way, 2], out, sem, along(which, 2 * step))
                send(sums.at[turn, which, block(which, other, 3 * step)],
                     far.at[turn, which, e, way, pl.ds(0, 2)], out, sem, along(which, step))
        for other in (True, False):
            e = int(other)
            for way, step in ((0, 1), (1, -1)):
                send(sums.at[turn, which, block(which, other, step)],
                     near.at[turn, which, e, way], out, sn_recv.at[turn, which, e], along(which, step))

    def scatter_relay(turn, which, other):
        e = int(other)
        for way, step in ((0, 1), (1, -1)):
            came = far.at[turn, which, e, way]
            awaits(came, sf_recv.at[turn, which, e, way])
            mine = sums.at[turn, which, block(which, other, 2 * step)]
            for owner in range(2):
                total = mine[owner].astype(F32) + came[owner].astype(F32)
                if owner == way:
                    total += came[2].astype(F32)
                relayed[turn, which, e, way, owner] = total.astype(BF16)
            send(relayed.at[turn, which, e, way], near.at[turn, which, e, 2 + way],
                 s_send.at[turn, which], sn_recv.at[turn, which, e], along(which, 2 * step))

    def scatter_sum(turn, which, other):
        e = int(other)
        awaits(near.at[turn, which, e], sn_recv.at[turn, which, e])
        into = x_out.at[turn, which] if other else pair_sum.at[turn, which]
        for owner in range(2):
            total = sums[turn, which, block(which, other, 0), owner].astype(F32)
            for part in range(4):
                total += near[turn, which, e, part, owner].astype(F32)
            into[owner] = total
        if other:
            send(x_out.at[turn, which], x_in.at[turn, which],
                 sx_send.at[turn, which], sx_recv.at[turn, which], across(which))

    def scatter_pair(turn, which):
        awaits(x_in.at[turn, which], sx_recv.at[turn, which])
        for owner in range(2):
            pair_sum[turn, which, owner] += x_in[turn, which, owner]
        send(pair_sum.at[turn, which, 1 - core], halves.at[turn, which, core],
             sm_send.at[turn, which], sm_recv.at[turn, which], mate)
        halves[turn, which, core] = pair_sum[turn, which, core]

    def scatter_end(turn, which):
        awaits(halves.at[turn, which, 1 - core], sm_recv.at[turn, which])
        return jnp.concatenate([halves[turn, which, 0], halves[turn, which, 1]], axis=1)

    def prepare():
        user_base = (row * BLOCKS + col) * ROWS
        item_base = (col * 2 * BLOCKS + row) * ROWS
        places = lax.broadcasted_iota(jnp.int32, (ROWS, uid_ref.shape[1]), 0)
        hot = jnp.where(places == uid_ref[...] - user_base, 1.0, 0.0).astype(F32)
        user_hot[...] = hot.astype(BF16)
        user_hot_t[...] = jnp.concatenate([hot] * 3, axis=0).T.astype(BF16)
        hot = jnp.where(places == nid_ref[...] - item_base, 1.0, 0.0).astype(F32)
        hot = hot - jnp.where(places == pid_ref[...] - item_base, 1.0, 0.0).astype(F32)
        item_hot[...] = hot.astype(BF16)
        item_hot_t[...] = jnp.concatenate([hot] * 3, axis=0).T.astype(BF16)

    both = (ITEMS, USERS)

    def propagate(turn):
        for which in both:
            gather_mate(turn, which)
        if turn == 0:
            send(tiles_hbm, tiles.at[core], tile_send, tile_recv, mate)
            send(meta.at[core], meta.at[core], meta_send, meta_recv, mate)
        for which in both:
            gather_own(turn, which)
        if turn == 0:
            prepare()
        for which in both:
            gather_across(turn, which)
        for which in both:
            gather_relay(turn, which, False)
        if turn == 0:
            load.wait()
            awaits(meta.at[1 - core], meta_recv)
            fill = pltpu.make_async_copy(meta, meta_smem, meta_sem)
            fill.start()
            fill.wait()
        for which in both:
            gather_relay(turn, which, True)
        if turn == 0:
            awaits(tiles.at[1 - core], tile_recv)
            for cell in range(2):
                for slot in range(SLOTS):
                    tiles_t[cell, slot] = tiles[cell, slot].T
        gather_end(turn, ITEMS)
        spread_users(turn)
        scatter_start(turn, USERS)
        gather_end(turn, USERS)
        spread_items(turn)
        scatter_start(turn, ITEMS)
        for other in (True, False):
            for which in (USERS, ITEMS):
                scatter_relay(turn, which, other)
        for other in (True, False):
            for which in (USERS, ITEMS):
                scatter_sum(turn, which, other)
        for which in (USERS, ITEMS):
            scatter_pair(turn, which)
        return scatter_end(turn, USERS), scatter_end(turn, ITEMS)

    own_rows(0, ITEMS, items_ref[...])
    own_rows(0, USERS, users_ref[...])
    pl.semaphore_wait(barrier, len(peers))
    first_users, first_items = propagate(0)
    final_users = 0.5 * (users_ref[...] + first_users)
    final_items = 0.5 * (items_ref[...] + first_items)

    dot = functools.partial(jnp.dot, preferred_element_type=F32)
    chosen = dot(user_hot_t[...], split(final_users, 3))
    against = dot(item_hot_t[...], split(final_items, 3))
    score = -jnp.sum(chosen * against, axis=1, keepdims=True)
    back = jax.nn.sigmoid(-score)
    hot = user_hot[...]
    grad_users = dot(jnp.concatenate([hot] * 3, axis=1), split(back * against, 3))
    hot = item_hot[...]
    grad_items = dot(jnp.concatenate([hot] * 3, axis=1), split(back * chosen, 3))

    own_rows(1, ITEMS, grad_items)
    own_rows(1, USERS, grad_users)
    back_users, back_items = propagate(1)
    out_users_ref[...] = 0.5 * grad_users + 0.5 * back_users
    out_items_ref[...] = 0.5 * grad_items + 0.5 * back_items

    sent(tiles_hbm, tile_send)
    sent(meta.at[core], meta_send)
    for turn in range(2):
        for which in (USERS, ITEMS):
            sent(stage.at[turn, which, core], gm_send.at[turn, which])
            sent(sums.at[turn, which, pl.ds(0, 15)], gb_send.at[turn, which])
            sent(sums.at[turn, which, pl.ds(0, 14)], s_send.at[turn, which])
            sent(x_out.at[turn, which], sx_send.at[turn, which])
            sent(pair_sum.at[turn, which, core], sm_send.at[turn, which])


def on_device(users, items, tiles, tile_pos, tile_count, user_ids, pos_ids, neg_ids):
    vmem = pl.BlockSpec(memory_space=pltpu.VMEM)
    smem = pl.BlockSpec(memory_space=pltpu.SMEM)
    dma = pltpu.SemaphoreType.DMA
    batch = user_ids.shape[0]
    cut = (2, ROWS, HALF)
    return pl.pallas_call(
        kernel,
        out_shape=(
            jax.ShapeDtypeStruct((ROWS, WIDTH), F32),
            jax.ShapeDtypeStruct((ROWS, WIDTH), F32),
        ),
        in_specs=[vmem, vmem, smem, smem, vmem, vmem, vmem, pl.BlockSpec(memory_space=pl.ANY)],
        out_specs=(vmem, vmem),
        scratch_shapes=[
            pltpu.VMEM((2, SLOTS, TILE, TILE), BF16),
            pltpu.VMEM((2, SLOTS, TILE, TILE), BF16),
            pltpu.VMEM((2, 8, HALF), jnp.int32),
            pltpu.SMEM((2, 8, HALF), jnp.int32),
            pltpu.VMEM((ROWS, batch), BF16),
            pltpu.VMEM((ROWS, batch), BF16),
            pltpu.VMEM((batch, 3 * ROWS), BF16),
            pltpu.VMEM((batch, 3 * ROWS), BF16),
            pltpu.VMEM((4, 4) + cut, BF16),
            pltpu.VMEM((4, 4) + cut, BF16),
            pltpu.VMEM((8, 2) + cut, BF16),
            pltpu.VMEM((8, 2) + cut, BF16),
            pltpu.VMEM((2, 2) + cut, BF16),
            pltpu.VMEM((2 * SLOTS, TILE, HALF), F32),
            pltpu.VMEM((2, 2, BLOCKS) + cut, BF16),
            pltpu.VMEM((2, 2, 2, 2, 3, ROWS, HALF), BF16),
            pltpu.VMEM((2, 2, 2, 2) + cut, BF16),
            pltpu.VMEM((2, 2, 2, 4) + cut, BF16),
            pltpu.VMEM((2, 2) + cut, F32),
            pltpu.VMEM((2, 2) + cut, F32),
            pltpu.VMEM((2, 2) + cut, F32),
            pltpu.VMEM((2, 2) + cut, F32),
            dma,
            dma,
            dma,
            dma,
            dma,
            dma,
            dma((2, 2)),
            dma((2, 2)),
            dma((2, 2)),
            dma((2, 2, 2, 2)),
            dma((2, 2)),
            dma((2, 2)),
            dma((2, 2, 2, 2)),
            dma((2, 2, 2)),
            dma((2, 2)),
            dma((2, 2)),
            dma((2, 2)),
            dma((2, 2)),
            dma((2, 2)),
        ],
        compiler_params=pltpu.CompilerParams(
            collective_id=0, has_side_effects=True, vmem_limit_bytes=40 << 20
        ),
        name="propagation_layer",
    )(
        users,
        items,
        tile_pos.reshape(1, SLOTS),
        tile_count,
        user_ids.reshape(1, batch),
        pos_ids.reshape(1, batch),
        neg_ids.reshape(1, batch),
        tiles.reshape(SLOTS, TILE, TILE),
    )


def solution(mesh):
    placed = (
        P(("row", "col"), None),
        P(("col", "row"), None),
        P("row", "col", None, None, None),
        P("row", "col", None),
        P("row", "col"),
        P(("row", "col")),
        P(("row", "col")),
        P(("row", "col")),
    )
    return jax.shard_map(
        on_device,
        mesh=mesh,
        in_specs=placed,
        out_specs=(P(("row", "col"), None), P(("col", "row"), None)),
        check_vma=False,
    )
```

time: 1030 us -> 77.1 us (0.07)
  waiting for transfers between devices: 902 us -> 0 us
  blocking collectives: 74.4 us -> 0 us
  Pallas kernels: 0 us -> 70.8 us
  between operations: 14.4 us -> 1.32 us
    psum x4 -> x0, waiting for transfers between devices: 838 us -> none  [the longest x2 488 us: reduce_items(): summed = lax.psum(partial_value, 'row')]
    all_gather x2 -> x0, blocking collectives: 74.4 us -> none  [spread(): lax.all_gather(user_side, 'col', axis=0, tiled=True)]
    pallas_call x0 -> x1, Pallas kernels: none -> 70.8 us  [on_device(): pl.pallas_call(kernel, out_shape=(jax.ShapeDtypeStruct((ROWS, WIDTH), F32...]
    all_gather x2 -> x0, waiting for transfers between devices: 64.4 us -> none  [spread(): lax.all_gather(item_side, 'row', axis=0, tiled=True)]
  transfers between devices with their start and end apart: 6 -> 0, of which waited for: 6 -> 0; matrix products, arithmetic and copies ran while one was open for 0% -> 0% of each run, Pallas kernels for 0% -> 0%
where the time goes in v2:
time: 77.1 us; the launch traced here: 76.8 us
  Pallas kernels  70.8 us (92%)
  local copies, waits for them, and re-layouts  4.66 us (6%)
  between operations  1.32 us (2%)
    pallas_call x1, Pallas kernels, on_device(): pl.pallas_call(kernel, out_shape=(jax.ShapeDtypeStruct((ROWS, WIDTH), F32...  70.8 us
    unnamed x16, local copies, waits for them, and re-layouts  4.66 us

profile of v2, /device:TPU:1, one launch (start us, length us, event | category | flops | bytes accessed | tf_op | source)
XLA Modules:
  0.0 76.8 jit_solution(15319735185254128213)
XLA Ops:
  1.3 0.0 copy-start.4
  1.3 0.0 copy-start.5
  1.3 0.0 copy-start.3
  1.3 0.0 copy-start.6
  1.3 0.6 copy-done.4
  2.0 0.0 copy-done.5
  2.0 0.0 copy-done.3
  2.0 0.0 copy-done.6
  2.0 0.0 copy-start
  2.0 1.0 %copy-done = bf16[1,1,4,256,256]{4,3,2,1,0:T(8,128)(2,1)S(1)} copy-done((bf16[1,1,4,256,256]{4,3,2,1,0:T(8,128)(2,1)S(1)}, bf16[1,1,4,256,256]{4,3,2,1,0:T(8,128)(2,1)}, u32[]{:S(2)}) %copy-start) | copy-done | bytes 524312
  3.0 0.0 copy-start.1
  3.0 0.8 %copy-done.1 = f32[64,256]{1,0:T(8,128)S(1)} copy-done((f32[64,256]{1,0:T(8,128)S(1)}, f32[64,256]{1,0:T(8,128)}, u32[]{:S(2)}) %copy-start.1) | copy-done | bytes 65560
  3.9 0.0 copy-start.2
  3.9 0.8 %copy-done.2 = f32[64,256]{1,0:T(8,128)S(1)} copy-done((f32[64,256]{1,0:T(8,128)S(1)}, f32[64,256]{1,0:T(8,128)}, u32[]{:S(2)}) %copy-start.2) | copy-done | bytes 65560
  4.7 70.8 %propagation_layer.1 = (f32[64,256]{1,0:T(8,128)S(1)}, f32[64,256]{1,0:T(8,128)S(1)}) custom-call(f32[64,256]{1,0:T(8,128)S(1)} %copy-done.1, f32[64,256]{1,0:T(8,128)S(1)} %copy-done.2, s32[1,4]{1,0:T(1,128)S(1)} %bitcast.9, s32[1,1]{1,0:T(1,128)S(6)} %copy.12.count_ref, s32[1,256]{1,0:T(1,128)S(1)} %bitcast.6, s32[1,256]{1,0:T(1,128)S(1)} %bitcast.7, ...), custom_call_target="tpu_custom_call" | custom-call | tf_op jit(solution)/shard_map/propagation_layer/pallas_call | solution.py:388
  75.5 0.6 copy.13
  76.2 0.6 copy.14
Async XLA Ops:
  1.3 0.7 copy-start.4
  1.3 0.7 copy-start.5
  1.3 0.7 copy-start.3
  1.3 0.7 copy-start.6
  2.0 1.0 %copy-start = (bf16[1,1,4,256,256]{4,3,2,1,0:T(8,128)(2,1)S(1)}, bf16[1,1,4,256,256]{4,3,2,1,0:T(8,128)(2,1)}, u32[]{:S(2)}) copy-start(bf16[1,1,4,256,256]{4,3,2,1,0:T(8,128)(2,1)} %param.10) | copy-start | bytes 1572868
  3.0 0.8 %copy-start.1 = (f32[64,256]{1,0:T(8,128)S(1)}, f32[64,256]{1,0:T(8,128)}, u32[]{:S(2)}) copy-start(f32[64,256]{1,0:T(8,128)} %users_ref.1) | copy-start | bytes 196612
  3.9 0.8 %copy-start.2 = (f32[64,256]{1,0:T(8,128)S(1)}, f32[64,256]{1,0:T(8,128)}, u32[]{:S(2)}) copy-start(f32[64,256]{1,0:T(8,128)} %items_ref.1) | copy-start | bytes 196612

commit v3 on v2

--- a/solution.py
+++ b/solution.py
@@ -30,6 +30,16 @@
 
 
 def kernel(
+    users_hbm,
+    items_hbm,
+    pos_hbm,
+    count_hbm,
+    uid_hbm,
+    pid_hbm,
+    nid_hbm,
+    tiles_hbm,
+    out_users_ref,
+    out_items_ref,
     users_ref,
     items_ref,
     pos_ref,
@@ -37,9 +47,6 @@
     uid_ref,
     pid_ref,
     nid_ref,
-    tiles_hbm,
-    out_users_ref,
-    out_items_ref,
     tiles,
     tiles_t,
     meta,
@@ -57,11 +64,7 @@
     sums,
     far,
     relayed,
-    near,
-    x_out,
-    x_in,
-    pair_sum,
-    halves,
+    last,
     load_sem,
     tile_send,
     tile_recv,
@@ -70,17 +73,13 @@
     meta_recv,
     gm_send,
     gm_recv,
-    gx_recv,
     g2_recv,
     gb_send,
     gb_recv,
     sf_recv,
-    sn_recv,
+    sl_recv,
     s_send,
-    sx_send,
-    sx_recv,
     sm_send,
-    sm_recv,
 ):
     row = lax.axis_index("row")
     col = lax.axis_index("col")
@@ -90,20 +89,18 @@
     x_at = (col // RING, group // RING)
     ring_at = (lax.rem(col, RING), lax.rem(group, RING))
 
-    def device(which, x, ring):
-        if which == USERS:
-            return (row, x * RING + ring)
-        return ((x * RING + ring) * 2 + core, col)
-
-    def along(which, step):
-        return device(which, x_at[which], lax.rem(ring_at[which] + step + RING, RING))
-
-    def across(which):
-        return device(which, 1 - x_at[which], ring_at[which])
-
     def block(which, other, step):
         x = 1 - x_at[which] if other else x_at[which]
         return x * RING + lax.rem(ring_at[which] + step + RING, RING)
+
+    def device(which, other, step, to_core):
+        number = block(which, other, step)
+        if which == USERS:
+            return (group * 2 + to_core, number)
+        return (number * 2 + to_core, col)
+
+    def along(which, step):
+        return device(which, False, step, core)
 
     def send(source, target, send_sem, recv_sem, to):
         pltpu.make_async_remote_copy(
@@ -123,15 +120,32 @@
             device_id=mate, device_id_type=MESH,
         ).wait_send()
 
+    def load(number, source, target):
+        copy = pltpu.make_async_copy(source, target, load_sem.at[number])
+        copy.start()
+        return copy
+
+    items_load = load(0, items_hbm, items_ref)
+    users_load = load(1, users_hbm, users_ref)
+    pos_load = load(2, pos_hbm, pos_ref)
+    count_load = load(3, count_hbm, count_ref)
+    ids_load = [
+        load(4, uid_hbm, uid_ref), load(5, pid_hbm, pid_ref), load(6, nid_hbm, nid_ref)
+    ]
+    tiles_load = load(7, tiles_hbm, tiles.at[core])
+
     barrier = pltpu.get_barrier_semaphore()
+    far_steps = [(other, step) for step in (2, -2) for other in (True, False)]
+    near_steps = [(other, step) for step in (1, -1) for other in (True, False)] + [(True, 0)]
     peers = [mate]
     for which in (USERS, ITEMS):
-        peers += [across(which)] + [along(which, step) for step in (1, -1, 2, -2)]
+        for other, step in far_steps + near_steps:
+            peers += [device(which, other, step, to_core) for to_core in range(2)]
     for peer in peers:
         pl.semaphore_signal(barrier, 1, device_id=peer, device_id_type=MESH)
 
-    load = pltpu.make_async_copy(tiles_hbm, tiles.at[core], load_sem)
-    load.start()
+    pos_load.wait()
+    count_load.wait()
     filled = jnp.full((8, HALF), count_ref[0, 0], jnp.int32)
     slot_of = lax.broadcasted_iota(jnp.int32, (8, HALF), 0)
     placed = jnp.full((8, HALF), pos_ref[0, 0], jnp.int32)
@@ -151,28 +165,18 @@
         own = at_block(turn, which, block(which, False, 0))
         own[core] = stage[turn, which, core]
 
-    def gather_mate(turn, which):
-        own = at_block(turn, which, block(which, False, 0))
-        send(stage.at[turn, which, 1 - core], own.at[core],
+    def gather_start(turn, which):
+        own = at_block(turn, which, block(which, False, 0)).at[core]
+        for other, step in far_steps + near_steps:
+            if abs(step) == 2:
+                sem = g2_recv.at[turn, which, int(other), int(step < 0)]
+            else:
+                sem = gb_recv.at[turn, which]
+            for to_core in range(2):
+                send(stage.at[turn, which, to_core], own, gb_send.at[turn, which], sem,
+                     device(which, other, step, to_core))
+        send(stage.at[turn, which, 1 - core], own,
              gm_send.at[turn, which], gm_recv.at[turn, which], mate)
-
-    def gather_block(turn, which, other):
-        here = at_block(turn, which, block(which, other, 0))
-        for step in (2, -2):
-            send(here, here, gb_send.at[turn, which],
-                 g2_recv.at[turn, which, int(other), int(step < 0)], along(which, step))
-        for step in (1, -1):
-            send(here, here, gb_send.at[turn, which], gb_recv.at[turn, which], along(which, step))
-
-    def gather_own(turn, which):
-        own = at_block(turn, which, block(which, False, 0))
-        awaits(own.at[1 - core], gm_recv.at[turn, which])
-        send(own, own, gb_send.at[turn, which], gx_recv.at[turn, which], across(which))
-        gather_block(turn, which, False)
-
-    def gather_across(turn, which):
-        awaits(at_block(turn, which, block(which, True, 0)), gx_recv.at[turn, which])
-        gather_block(turn, which, True)
 
     def gather_relay(turn, which, other):
         for way, step in ((0, 1), (1, -1)):
@@ -183,7 +187,9 @@
             send(here, here, gb_send.at[turn, which], gb_recv.at[turn, which], along(which, step))
 
     def gather_end(turn, which):
-        awaits(sums.at[turn, which, pl.ds(0, 10)], gb_recv.at[turn, which])
+        awaits(sums.at[turn, which, pl.ds(0, 11)], gb_recv.at[turn, which])
+        own = at_block(turn, which, block(which, False, 0))
+        awaits(own.at[1 - core], gm_recv.at[turn, which])
 
     def marks(cell, slot):
         return meta[cell, pl.ds(slot, 1), :]
@@ -243,11 +249,17 @@
                      far.at[turn, which, e, way, 2], out, sem, along(which, 2 * step))
                 send(sums.at[turn, which, block(which, other, 3 * step)],
                      far.at[turn, which, e, way, pl.ds(0, 2)], out, sem, along(which, step))
-        for other in (True, False):
-            e = int(other)
-            for way, step in ((0, 1), (1, -1)):
-                send(sums.at[turn, which, block(which, other, step)],
-                     near.at[turn, which, e, way], out, sn_recv.at[turn, which, e], along(which, step))
+        for other, step in near_steps:
+            part = 0 if step == 0 else 1 + int(step < 0)
+            for to_core in range(2):
+                send_last(turn, which, other, step, part, to_core,
+                          sums.at[turn, which, block(which, other, step), to_core])
+        send(sums.at[turn, which, block(which, False, 0), 1 - core],
+             last.at[turn, which, core * 10], sm_send.at[turn, which], sl_recv.at[turn, which], mate)
+
+    def send_last(turn, which, other, step, part, to_core, source):
+        send(source, last.at[turn, which, core * 10 + int(other) * 5 + part],
+             s_send.at[turn, which], sl_recv.at[turn, which], device(which, other, step, to_core))
 
     def scatter_relay(turn, which, other):
         e = int(other)
@@ -260,33 +272,20 @@
                 if owner == way:
                     total += came[2].astype(F32)
                 relayed[turn, which, e, way, owner] = total.astype(BF16)
-            send(relayed.at[turn, which, e, way], near.at[turn, which, e, 2 + way],
-                 s_send.at[turn, which], sn_recv.at[turn, which, e], along(which, 2 * step))
-
-    def scatter_sum(turn, which, other):
-        e = int(other)
-        awaits(near.at[turn, which, e], sn_recv.at[turn, which, e])
-        into = x_out.at[turn, which] if other else pair_sum.at[turn, which]
-        for owner in range(2):
-            total = sums[turn, which, block(which, other, 0), owner].astype(F32)
-            for part in range(4):
-                total += near[turn, which, e, part, owner].astype(F32)
-            into[owner] = total
-        if other:
-            send(x_out.at[turn, which], x_in.at[turn, which],
-                 sx_send.at[turn, which], sx_recv.at[turn, which], across(which))
-
-    def scatter_pair(turn, which):
-        awaits(x_in.at[turn, which], sx_recv.at[turn, which])
-        for owner in range(2):
-            pair_sum[turn, which, owner] += x_in[turn, which, owner]
-        send(pair_sum.at[turn, which, 1 - core], halves.at[turn, which, core],
-             sm_send.at[turn, which], sm_recv.at[turn, which], mate)
-        halves[turn, which, core] = pair_sum[turn, which, core]
+            for to_core in range(2):
+                send_last(turn, which, other, 2 * step, 3 + way, to_core,
+                          relayed.at[turn, which, e, way, to_core])
 
     def scatter_end(turn, which):
-        awaits(halves.at[turn, which, 1 - core], sm_recv.at[turn, which])
-        return jnp.concatenate([halves[turn, which, 0], halves[turn, which, 1]], axis=1)
+        awaits(last.at[turn, which, pl.ds(0, 19)], sl_recv.at[turn, which])
+        last[turn, which, core * 10] = sums[turn, which, block(which, False, 0), core]
+        sides = []
+        for side in range(2):
+            total = last[turn, which, side * 10].astype(F32)
+            for part in range(1, 10):
+                total += last[turn, which, side * 10 + part].astype(F32)
+            sides.append(total)
+        return jnp.concatenate(sides, axis=1)
 
     def prepare():
         user_base = (row * BLOCKS + col) * ROWS
@@ -304,27 +303,23 @@
 
     def propagate(turn):
         for which in both:
-            gather_mate(turn, which)
+            gather_start(turn, which)
         if turn == 0:
             send(tiles_hbm, tiles.at[core], tile_send, tile_recv, mate)
             send(meta.at[core], meta.at[core], meta_send, meta_recv, mate)
-        for which in both:
-            gather_own(turn, which)
-        if turn == 0:
+            for copy in ids_load:
+                copy.wait()
             prepare()
         for which in both:
-            gather_across(turn, which)
+            gather_relay(turn, which, False)
         for which in both:
-            gather_relay(turn, which, False)
+            gather_relay(turn, which, True)
         if turn == 0:
-            load.wait()
+            tiles_load.wait()
             awaits(meta.at[1 - core], meta_recv)
             fill = pltpu.make_async_copy(meta, meta_smem, meta_sem)
             fill.start()
             fill.wait()
-        for which in both:
-            gather_relay(turn, which, True)
-        if turn == 0:
             awaits(tiles.at[1 - core], tile_recv)
             for cell in range(2):
                 for slot in range(SLOTS):
@@ -338,14 +333,11 @@
         for other in (True, False):
             for which in (USERS, ITEMS):
                 scatter_relay(turn, which, other)
-        for other in (True, False):
-            for which in (USERS, ITEMS):
-                scatter_sum(turn, which, other)
-        for which in (USERS, ITEMS):
-            scatter_pair(turn, which)
         return scatter_end(turn, USERS), scatter_end(turn, ITEMS)
 
+    items_load.wait()
     own_rows(0, ITEMS, items_ref[...])
+    users_load.wait()
     own_rows(0, USERS, users_ref[...])
     pl.semaphore_wait(barrier, len(peers))
     first_users, first_items = propagate(0)
@@ -374,14 +366,12 @@
         for which in (USERS, ITEMS):
             sent(stage.at[turn, which, core], gm_send.at[turn, which])
             sent(sums.at[turn, which, pl.ds(0, 15)], gb_send.at[turn, which])
-            sent(sums.at[turn, which, pl.ds(0, 14)], s_send.at[turn, which])
-            sent(x_out.at[turn, which], sx_send.at[turn, which])
-            sent(pair_sum.at[turn, which, core], sm_send.at[turn, which])
+            sent(sums.at[turn, which, pl.ds(0, 15)], s_send.at[turn, which])
+            sent(stage.at[turn, which, core], sm_send.at[turn, which])
 
 
 def on_device(users, items, tiles, tile_pos, tile_count, user_ids, pos_ids, neg_ids):
     vmem = pl.BlockSpec(memory_space=pltpu.VMEM)
-    smem = pl.BlockSpec(memory_space=pltpu.SMEM)
     dma = pltpu.SemaphoreType.DMA
     batch = user_ids.shape[0]
     cut = (2, ROWS, HALF)
@@ -391,9 +381,16 @@
             jax.ShapeDtypeStruct((ROWS, WIDTH), F32),
             jax.ShapeDtypeStruct((ROWS, WIDTH), F32),
         ),
-        in_specs=[vmem, vmem, smem, smem, vmem, vmem, vmem, pl.BlockSpec(memory_space=pl.ANY)],
+        in_specs=[pl.BlockSpec(memory_space=pl.ANY)] * 8,
         out_specs=(vmem, vmem),
         scratch_shapes=[
+            pltpu.VMEM((ROWS, WIDTH), F32),
+            pltpu.VMEM((ROWS, WIDTH), F32),
+            pltpu.SMEM((1, SLOTS), jnp.int32),
+            pltpu.SMEM((1, 1), jnp.int32),
+            pltpu.VMEM((1, batch), jnp.int32),
+            pltpu.VMEM((1, batch), jnp.int32),
+            pltpu.VMEM((1, batch), jnp.int32),
             pltpu.VMEM((2, SLOTS, TILE, TILE), BF16),
             pltpu.VMEM((2, SLOTS, TILE, TILE), BF16),
             pltpu.VMEM((2, 8, HALF), jnp.int32),
@@ -411,33 +408,25 @@
             pltpu.VMEM((2, 2, BLOCKS) + cut, BF16),
             pltpu.VMEM((2, 2, 2, 2, 3, ROWS, HALF), BF16),
             pltpu.VMEM((2, 2, 2, 2) + cut, BF16),
-            pltpu.VMEM((2, 2, 2, 4) + cut, BF16),
-            pltpu.VMEM((2, 2) + cut, F32),
-            pltpu.VMEM((2, 2) + cut, F32),
-            pltpu.VMEM((2, 2) + cut, F32),
-            pltpu.VMEM((2, 2) + cut, F32),
+            pltpu.VMEM((2, 2, 20, ROWS, HALF), BF16),
+            dma((8,)),
             dma,
             dma,
             dma,
             dma,
             dma,
-            dma,
-            dma((2, 2)),
             dma((2, 2)),
             dma((2, 2)),
             dma((2, 2, 2, 2)),
             dma((2, 2)),
             dma((2, 2)),
             dma((2, 2, 2, 2)),
-            dma((2, 2, 2)),
-            dma((2, 2)),
-            dma((2, 2)),
             dma((2, 2)),
             dma((2, 2)),
             dma((2, 2)),
         ],
         compiler_params=pltpu.CompilerParams(
-            collective_id=0, has_side_effects=True, vmem_limit_bytes=40 << 20
+            collective_id=0, has_side_effects=True, vmem_limit_bytes=60 << 20
         ),
         name="propagation_layer",
     )(

time: 77.1 us -> 67.1 us (0.87)
  Pallas kernels: 70.8 us -> 63.5 us
  local copies, waits for them, and re-layouts: 4.66 us -> 2.14 us
    pallas_call x1, Pallas kernels: 70.8 us -> 63.5 us  [on_device(): pl.pallas_call(kernel, out_shape=(jax.ShapeDtypeStruct((ROWS, WIDTH), F32...]
    unnamed x16 -> x4, local copies, waits for them, and re-layouts: 4.66 us -> 2.14 us
where the time goes in v3:
time: 67.1 us; the launch traced here: 66.9 us
  Pallas kernels  63.5 us (95%)
  local copies, waits for them, and re-layouts  2.14 us (3%)
  between operations  1.29 us (2%)
    pallas_call x1, Pallas kernels, on_device(): pl.pallas_call(kernel, out_shape=(jax.ShapeDtypeStruct((ROWS, WIDTH), F32...  63.5 us
    unnamed x4, local copies, waits for them, and re-layouts  2.14 us

profile of v3, /device:TPU:1, one launch (start us, length us, event | category | flops | bytes accessed | tf_op | source)
XLA Modules:
  0.0 66.9 jit_solution(9410956119387634559)
XLA Ops:
  1.3 63.5 %propagation_layer.1 = (f32[64,256]{1,0:T(8,128)}, f32[64,256]{1,0:T(8,128)}) custom-call(f32[64,256]{1,0:T(8,128)} %users_hbm.1, f32[64,256]{1,0:T(8,128)} %items_hbm.1, s32[1,4]{1,0:T(1,128)} %bitcast.9, s32[1,1]{1,0:T(1,128)S(6)} %copy.12.count_hbm, s32[1,256]{1,0:T(1,128)} %bitcast.6, s32[1,256]{1,0:T(1,128)} %bitcast.7, s32[1,256]{1,0:T(1,128)} %bitcast.8, ...), custom_call_target="tpu_custom_call" | custom-call | tf_op jit(solution)/shard_map/propagation_layer/pallas_call | solution.py:378
  64.8 0.0 copy-start
  64.8 1.5 %copy.13 = f32[64,256]{1,0:T(8,128)} copy(f32[64,256]{1,0:T(8,128)} %get-tuple-element.4) | data formatting | bytes 131072
  66.3 0.0 copy-done
  66.3 0.6 copy.14
Async XLA Ops:
  64.8 1.5 %copy-start = (f32[64,256]{1,0:T(8,128)S(1)}, f32[64,256]{1,0:T(8,128)}, u32[]{:S(2)}) copy-start(f32[64,256]{1,0:T(8,128)} %get-tuple-element.5) | copy-start | bytes 196612

commit v4 on v3

--- a/solution.py
+++ b/solution.py
@@ -38,8 +38,7 @@
     pid_hbm,
     nid_hbm,
     tiles_hbm,
-    out_users_ref,
-    out_items_ref,
+    out_ref,
     users_ref,
     items_ref,
     pos_ref,
@@ -61,8 +60,11 @@
     item_panel_1,
     stage,
     prod,
+    exact,
     sums,
     far,
+    cross,
+    paired,
     relayed,
     last,
     load_sem,
@@ -73,10 +75,12 @@
     meta_recv,
     gm_send,
     gm_recv,
+    g1_recv,
     g2_recv,
     gb_send,
     gb_recv,
     sf_recv,
+    sx_recv,
     sl_recv,
     s_send,
     sm_send,
@@ -136,7 +140,7 @@
 
     barrier = pltpu.get_barrier_semaphore()
     far_steps = [(other, step) for step in (2, -2) for other in (True, False)]
-    near_steps = [(other, step) for step in (1, -1) for other in (True, False)] + [(True, 0)]
+    near_steps = [(False, 1), (False, -1), (True, 0)]
     peers = [mate]
     for which in (USERS, ITEMS):
         for other, step in far_steps + near_steps:
@@ -170,6 +174,8 @@
         for other, step in far_steps + near_steps:
             if abs(step) == 2:
                 sem = g2_recv.at[turn, which, int(other), int(step < 0)]
+            elif abs(step) == 1:
+                sem = g1_recv.at[turn, which, int(step < 0)]
             else:
                 sem = gb_recv.at[turn, which]
             for to_core in range(2):
@@ -186,8 +192,15 @@
             send(part, part, gb_send.at[turn, which], gb_recv.at[turn, which], along(which, 2 * step))
             send(here, here, gb_send.at[turn, which], gb_recv.at[turn, which], along(which, step))
 
+    def gather_cross(turn, which):
+        for way, step in ((0, 1), (1, -1)):
+            here = at_block(turn, which, block(which, False, -step))
+            awaits(here, g1_recv.at[turn, which, way])
+            send(here, here, gb_send.at[turn, which], gb_recv.at[turn, which],
+                 device(which, True, 0, core))
+
     def gather_end(turn, which):
-        awaits(sums.at[turn, which, pl.ds(0, 11)], gb_recv.at[turn, which])
+        awaits(sums.at[turn, which, pl.ds(0, 9)], gb_recv.at[turn, which])
         own = at_block(turn, which, block(which, False, 0))
         awaits(own.at[1 - core], gm_recv.at[turn, which])
 
@@ -210,6 +223,7 @@
                 for slot in range(SLOTS):
                     weight = jnp.where((marks(cell, slot) >> 3) == number // 4, 1.0, 0.0)
                     total += weight.astype(F32) * prod[cell * SLOTS + slot, start, :]
+                exact[USERS, number, cell] = total
                 sums[turn, USERS, number, cell] = total.astype(BF16)
             return carry
 
@@ -234,6 +248,7 @@
                     for slot in range(SLOTS):
                         weight = jnp.where((marks(cell, slot) & 71) == number // 2, 1.0, 0.0)
                         total += weight.astype(F32) * prod[cell * SLOTS + slot, start, :]
+                exact[ITEMS, number, owner] = total
                 sums[turn, ITEMS, number, owner] = total.astype(BF16)
             return carry
 
@@ -249,41 +264,54 @@
                      far.at[turn, which, e, way, 2], out, sem, along(which, 2 * step))
                 send(sums.at[turn, which, block(which, other, 3 * step)],
                      far.at[turn, which, e, way, pl.ds(0, 2)], out, sem, along(which, step))
-        for other, step in near_steps:
-            part = 0 if step == 0 else 1 + int(step < 0)
+        for way, step in ((0, 1), (1, -1)):
+            send(sums.at[turn, which, block(which, True, step)], cross.at[turn, which, way],
+                 out, sx_recv.at[turn, which], device(which, True, 0, core))
+        for to_core in range(2):
+            send_last(turn, which, True, 0, 5, to_core,
+                      sums.at[turn, which, block(which, True, 0), to_core])
+        send(sums.at[turn, which, block(which, False, 0), 1 - core],
+             last.at[turn, which, core * 8], sm_send.at[turn, which], sl_recv.at[turn, which], mate)
+
+    def send_last(turn, which, other, step, part, to_core, source):
+        send(source, last.at[turn, which, core * 8 + part],
+             s_send.at[turn, which], sl_recv.at[turn, which], device(which, other, step, to_core))
+
+    def scatter_near(turn, which):
+        awaits(cross.at[turn, which], sx_recv.at[turn, which])
+        for way, step in ((0, 1), (1, -1)):
+            number = block(which, False, step)
             for to_core in range(2):
-                send_last(turn, which, other, step, part, to_core,
-                          sums.at[turn, which, block(which, other, step), to_core])
-        send(sums.at[turn, which, block(which, False, 0), 1 - core],
-             last.at[turn, which, core * 10], sm_send.at[turn, which], sl_recv.at[turn, which], mate)
-
-    def send_last(turn, which, other, step, part, to_core, source):
-        send(source, last.at[turn, which, core * 10 + int(other) * 5 + part],
-             s_send.at[turn, which], sl_recv.at[turn, which], device(which, other, step, to_core))
+                total = exact[which, number, to_core] + cross[turn, which, way, to_core].astype(F32)
+                paired[turn, which, way, to_core] = total.astype(BF16)
+            for to_core in range(2):
+                send_last(turn, which, False, step, 1 + way, to_core,
+                          paired.at[turn, which, way, to_core])
 
     def scatter_relay(turn, which, other):
         e = int(other)
         for way, step in ((0, 1), (1, -1)):
             came = far.at[turn, which, e, way]
             awaits(came, sf_recv.at[turn, which, e, way])
-            mine = sums.at[turn, which, block(which, other, 2 * step)]
+            mine = exact.at[which, block(which, other, 2 * step)]
             for owner in range(2):
-                total = mine[owner].astype(F32) + came[owner].astype(F32)
+                total = mine[owner] + came[owner].astype(F32)
                 if owner == way:
                     total += came[2].astype(F32)
                 relayed[turn, which, e, way, owner] = total.astype(BF16)
             for to_core in range(2):
-                send_last(turn, which, other, 2 * step, 3 + way, to_core,
+                send_last(turn, which, other, 2 * step, (6 if other else 3) + way, to_core,
                           relayed.at[turn, which, e, way, to_core])
 
     def scatter_end(turn, which):
-        awaits(last.at[turn, which, pl.ds(0, 19)], sl_recv.at[turn, which])
-        last[turn, which, core * 10] = sums[turn, which, block(which, False, 0), core]
+        awaits(last.at[turn, which, pl.ds(0, 15)], sl_recv.at[turn, which])
+        last[turn, which, core * 8] = jnp.zeros((ROWS, HALF), BF16)
+        own = exact[which, block(which, False, 0), core]
         sides = []
         for side in range(2):
-            total = last[turn, which, side * 10].astype(F32)
-            for part in range(1, 10):
-                total += last[turn, which, side * 10 + part].astype(F32)
+            total = jnp.where(core == side, own, 0.0)
+            for part in range(8):
+                total += last[turn, which, side * 8 + part].astype(F32)
             sides.append(total)
         return jnp.concatenate(sides, axis=1)
 
@@ -302,8 +330,6 @@
     both = (ITEMS, USERS)
 
     def propagate(turn):
-        for which in both:
-            gather_start(turn, which)
         if turn == 0:
             send(tiles_hbm, tiles.at[core], tile_send, tile_recv, mate)
             send(meta.at[core], meta.at[core], meta_send, meta_recv, mate)
@@ -312,6 +338,8 @@
             prepare()
         for which in both:
             gather_relay(turn, which, False)
+        for which in both:
+            gather_cross(turn, which)
         for which in both:
             gather_relay(turn, which, True)
         if turn == 0:
@@ -333,6 +361,8 @@
         for other in (True, False):
             for which in (USERS, ITEMS):
                 scatter_relay(turn, which, other)
+        for which in (USERS, ITEMS):
+            scatter_near(turn, which)
         return scatter_end(turn, USERS), scatter_end(turn, ITEMS)
 
     items_load.wait()
@@ -340,6 +370,8 @@
     users_load.wait()
     own_rows(0, USERS, users_ref[...])
     pl.semaphore_wait(barrier, len(peers))
+    for which in both:
+        gather_start(0, which)
     first_users, first_items = propagate(0)
     final_users = 0.5 * (users_ref[...] + first_users)
     final_items = 0.5 * (items_ref[...] + first_items)
@@ -350,15 +382,16 @@
     score = -jnp.sum(chosen * against, axis=1, keepdims=True)
     back = jax.nn.sigmoid(-score)
     hot = user_hot[...]
-    grad_users = dot(jnp.concatenate([hot] * 3, axis=1), split(back * against, 3))
+    grad_users = dot(jnp.concatenate([hot] * 2, axis=1), split(back * against, 2))
+    own_rows(1, USERS, grad_users)
+    gather_start(1, USERS)
     hot = item_hot[...]
-    grad_items = dot(jnp.concatenate([hot] * 3, axis=1), split(back * chosen, 3))
-
+    grad_items = dot(jnp.concatenate([hot] * 2, axis=1), split(back * chosen, 2))
     own_rows(1, ITEMS, grad_items)
-    own_rows(1, USERS, grad_users)
+    gather_start(1, ITEMS)
     back_users, back_items = propagate(1)
-    out_users_ref[...] = 0.5 * grad_users + 0.5 * back_users
-    out_items_ref[...] = 0.5 * grad_items + 0.5 * back_items
+    out_ref[0] = 0.5 * grad_users + 0.5 * back_users
+    out_ref[1] = 0.5 * grad_items + 0.5 * back_items
 
     sent(tiles_hbm, tile_send)
     sent(meta.at[core], meta_send)
@@ -375,14 +408,11 @@
     dma = pltpu.SemaphoreType.DMA
     batch = user_ids.shape[0]
     cut = (2, ROWS, HALF)
-    return pl.pallas_call(
+    out = pl.pallas_call(
         kernel,
-        out_shape=(
-            jax.ShapeDtypeStruct((ROWS, WIDTH), F32),
-            jax.ShapeDtypeStruct((ROWS, WIDTH), F32),
-        ),
+        out_shape=jax.ShapeDtypeStruct((2, ROWS, WIDTH), F32),
         in_specs=[pl.BlockSpec(memory_space=pl.ANY)] * 8,
-        out_specs=(vmem, vmem),
+        out_specs=vmem,
         scratch_shapes=[
             pltpu.VMEM((ROWS, WIDTH), F32),
             pltpu.VMEM((ROWS, WIDTH), F32),
@@ -405,10 +435,13 @@
             pltpu.VMEM((8, 2) + cut, BF16),
             pltpu.VMEM((2, 2) + cut, BF16),
             pltpu.VMEM((2 * SLOTS, TILE, HALF), F32),
+            pltpu.VMEM((2, BLOCKS) + cut, F32),
             pltpu.VMEM((2, 2, BLOCKS) + cut, BF16),
             pltpu.VMEM((2, 2, 2, 2, 3, ROWS, HALF), BF16),
+            pltpu.VMEM((2, 2, 2) + cut, BF16),
+            pltpu.VMEM((2, 2, 2) + cut, BF16),
             pltpu.VMEM((2, 2, 2, 2) + cut, BF16),
-            pltpu.VMEM((2, 2, 20, ROWS, HALF), BF16),
+            pltpu.VMEM((2, 2, 16, ROWS, HALF), BF16),
             dma((8,)),
             dma,
             dma,
@@ -417,10 +450,12 @@
             dma,
             dma((2, 2)),
             dma((2, 2)),
+            dma((2, 2, 2)),
             dma((2, 2, 2, 2)),
             dma((2, 2)),
             dma((2, 2)),
             dma((2, 2, 2, 2)),
+            dma((2, 2)),
             dma((2, 2)),
             dma((2, 2)),
             dma((2, 2)),
@@ -439,6 +474,7 @@
         neg_ids.reshape(1, batch),
         tiles.reshape(SLOTS, TILE, TILE),
     )
+    return out[0], out[1]
 
 
 def solution(mesh):

time: 67.1 us -> 65.6 us (0.978)
  Pallas kernels: 63.5 us -> 62.6 us
    unnamed x4 -> x0, local copies, waits for them, and re-layouts: 2.14 us -> none
    squeeze x0 -> x1, local copies, waits for them, and re-layouts: none -> 1.53 us  [on_device(): return (out[0], out[1])]
    pallas_call x1, Pallas kernels: 63.5 us -> 62.6 us  [on_device(): pl.pallas_call(kernel, out_shape=jax.ShapeDtypeStruct((2, ROWS, WIDTH), F...]
where the time goes in v4:
time: 65.6 us; the launch traced here: 65.4 us
  Pallas kernels  62.6 us (95%)
  local copies, waits for them, and re-layouts  1.53 us (2%)
  between operations  1.29 us (2%)
    pallas_call x1, Pallas kernels, on_device(): pl.pallas_call(kernel, out_shape=jax.ShapeDtypeStruct((2, ROWS, WIDTH), F...  62.6 us
    squeeze x1, local copies, waits for them, and re-layouts, on_device(): return (out[0], out[1])  1.53 us

profile of v4, /device:TPU:1, one launch (start us, length us, event | category | flops | bytes accessed | tf_op | source)
XLA Modules:
  0.0 65.4 jit_solution(1974326271549290744)
XLA Ops:
  1.3 62.6 %propagation_layer.1 = f32[2,64,256]{2,1,0:T(8,128)} custom-call(f32[64,256]{1,0:T(8,128)} %users_hbm.1, f32[64,256]{1,0:T(8,128)} %items_hbm.1, s32[1,4]{1,0:T(1,128)} %bitcast.13, s32[1,1]{1,0:T(1,128)S(6)} %copy.10.count_hbm, s32[1,256]{1,0:T(1,128)} %bitcast.10, s32[1,256]{1,0:T(1,128)} %bitcast.11, s32[1,256]{1,0:T(1,128)} %bitcast.12, ...), custom_call_target="tpu_custom_call" | custom-call | tf_op jit(solution)/shard_map/propagation_layer/pallas_call | solution.py:411
  63.9 1.5 %slice_bitcast_fusion = (f32[64,256]{1,0:T(8,128)}, f32[64,256]{1,0:T(8,128)}) fusion(f32[2,64,256]{2,1,0:T(8,128)} %propagation_layer.1), kind=kLoop, calls=%fused_computation | loop fusion | bytes 262144 | tf_op jit(solution)/shard_map/squeeze | solution.py:477

commit v5 on v4

--- a/solution.py
+++ b/solution.py
@@ -227,7 +227,7 @@
                 sums[turn, USERS, number, cell] = total.astype(BF16)
             return carry
 
-        lax.fori_loop(0, BLOCKS, add, 0)
+        lax.fori_loop(0, BLOCKS, add, 0, unroll=4)
 
     def spread_items(turn):
         panel = panels[turn][USERS]
@@ -252,7 +252,7 @@
                 sums[turn, ITEMS, number, owner] = total.astype(BF16)
             return carry
 
-        lax.fori_loop(0, BLOCKS, add, 0)
+        lax.fori_loop(0, BLOCKS, add, 0, unroll=4)
 
     def scatter_start(turn, which):
         out = s_send.at[turn, which]
@@ -401,6 +401,10 @@
             sent(sums.at[turn, which, pl.ds(0, 15)], gb_send.at[turn, which])
             sent(sums.at[turn, which, pl.ds(0, 15)], s_send.at[turn, which])
             sent(stage.at[turn, which, core], sm_send.at[turn, which])
+
+
+def in_hbm(value):
+    return pltpu.with_memory_space_constraint(value, pltpu.HBM)
 
 
 def on_device(users, items, tiles, tile_pos, tile_count, user_ids, pos_ids, neg_ids):
@@ -461,18 +465,18 @@
             dma((2, 2)),
         ],
         compiler_params=pltpu.CompilerParams(
-            collective_id=0, has_side_effects=True, vmem_limit_bytes=60 << 20
+            collective_id=0, has_side_effects=True, vmem_limit_bytes=40 << 20
         ),
         name="propagation_layer",
     )(
-        users,
-        items,
-        tile_pos.reshape(1, SLOTS),
+        in_hbm(users),
+        in_hbm(items),
+        in_hbm(tile_pos.reshape(1, SLOTS)),
         tile_count,
-        user_ids.reshape(1, batch),
-        pos_ids.reshape(1, batch),
-        neg_ids.reshape(1, batch),
-        tiles.reshape(SLOTS, TILE, TILE),
+        in_hbm(user_ids.reshape(1, batch)),
+        in_hbm(pos_ids.reshape(1, batch)),
+        in_hbm(neg_ids.reshape(1, batch)),
+        in_hbm(tiles.reshape(SLOTS, TILE, TILE)),
     )
     return out[0], out[1]
 

time: 65.6 us -> 63.5 us (0.968)
  Pallas kernels: 62.6 us -> 61.4 us
  local copies, waits for them, and re-layouts: 1.53 us -> 0.66 us
    pallas_call x1, Pallas kernels: 62.6 us -> 61.4 us  [on_device(): pl.pallas_call(kernel, out_shape=jax.ShapeDtypeStruct((2, ROWS, WIDTH), F...]
    squeeze x1, local copies, waits for them, and re-layouts: 1.53 us -> 0.66 us  [on_device(): return (out[0], out[1])]
where the time goes in v5:
time: 63.5 us; the launch traced here: 63.4 us
  Pallas kernels  61.4 us (97%)
  between operations  1.29 us (2%)
  local copies, waits for them, and re-layouts  0.66 us (1%)
    pallas_call x1, Pallas kernels, on_device(): pl.pallas_call(kernel, out_shape=jax.ShapeDtypeStruct((2, ROWS, WIDTH), F...  61.4 us

profile of v5, /device:TPU:1, one launch (start us, length us, event | category | flops | bytes accessed | tf_op | source)
XLA Modules:
  0.0 63.4 jit_solution(11760567172571348461)
XLA Ops:
  1.3 61.4 %propagation_layer.1 = f32[2,64,256]{2,1,0:T(8,128)S(1)} custom-call(f32[64,256]{1,0:T(8,128)} %users_hbm.1, f32[64,256]{1,0:T(8,128)} %items_hbm.1, s32[1,4]{1,0:T(1,128)} %bitcast.13, s32[1,1]{1,0:T(1,128)S(6)} %copy.10.count_hbm, s32[1,256]{1,0:T(1,128)} %bitcast.10, s32[1,256]{1,0:T(1,128)} %bitcast.11, s32[1,256]{1,0:T(1,128)} %bitcast.12, ...), custom_call_target="tpu_custom_call" | custom-call | tf_op jit(solution)/shard_map/propagation_layer/pallas_call | solution.py:415
  62.7 0.7 %slice_bitcast_fusion = (f32[64,256]{1,0:T(8,128)}, f32[64,256]{1,0:T(8,128)}) fusion(f32[2,64,256]{2,1,0:T(8,128)S(1)} %propagation_layer.1), kind=kLoop, calls=%fused_computation | loop fusion | bytes 262144 | tf_op jit(solution)/shard_map/squeeze | solution.py:481

commit v6 on v5

--- a/solution.py
+++ b/solution.py
@@ -327,6 +327,16 @@
         item_hot[...] = hot.astype(BF16)
         item_hot_t[...] = jnp.concatenate([hot] * 3, axis=0).T.astype(BF16)
 
+    def gather_sent(turn):
+        for which in (USERS, ITEMS):
+            sent(stage.at[turn, which, core], gm_send.at[turn, which])
+            sent(sums.at[turn, which, pl.ds(0, 15)], gb_send.at[turn, which])
+
+    def scatter_sent(turn):
+        for which in (USERS, ITEMS):
+            sent(sums.at[turn, which, pl.ds(0, 15)], s_send.at[turn, which])
+            sent(stage.at[turn, which, core], sm_send.at[turn, which])
+
     both = (ITEMS, USERS)
 
     def propagate(turn):
@@ -342,6 +352,11 @@
             gather_cross(turn, which)
         for which in both:
             gather_relay(turn, which, True)
+        if turn == 1:
+            sent(tiles_hbm, tile_send)
+            sent(meta.at[core], meta_send)
+            gather_sent(0)
+            scatter_sent(0)
         if turn == 0:
             tiles_load.wait()
             awaits(meta.at[1 - core], meta_recv)
@@ -363,7 +378,8 @@
                 scatter_relay(turn, which, other)
         for which in (USERS, ITEMS):
             scatter_near(turn, which)
-        return scatter_end(turn, USERS), scatter_end(turn, ITEMS)
+        if turn == 1:
+            gather_sent(1)
 
     items_load.wait()
     own_rows(0, ITEMS, items_ref[...])
@@ -372,12 +388,11 @@
     pl.semaphore_wait(barrier, len(peers))
     for which in both:
         gather_start(0, which)
-    first_users, first_items = propagate(0)
-    final_users = 0.5 * (users_ref[...] + first_users)
-    final_items = 0.5 * (items_ref[...] + first_items)
-
+    propagate(0)
     dot = functools.partial(jnp.dot, preferred_element_type=F32)
+    final_users = 0.5 * (users_ref[...] + scatter_end(0, USERS))
     chosen = dot(user_hot_t[...], split(final_users, 3))
+    final_items = 0.5 * (items_ref[...] + scatter_end(0, ITEMS))
     against = dot(item_hot_t[...], split(final_items, 3))
     score = -jnp.sum(chosen * against, axis=1, keepdims=True)
     back = jax.nn.sigmoid(-score)
@@ -389,18 +404,10 @@
     grad_items = dot(jnp.concatenate([hot] * 2, axis=1), split(back * chosen, 2))
     own_rows(1, ITEMS, grad_items)
     gather_start(1, ITEMS)
-    back_users, back_items = propagate(1)
-    out_ref[0] = 0.5 * grad_users + 0.5 * back_users
-    out_ref[1] = 0.5 * grad_items + 0.5 * back_items
-
-    sent(tiles_hbm, tile_send)
-    sent(meta.at[core], meta_send)
-    for turn in range(2):
-        for which in (USERS, ITEMS):
-            sent(stage.at[turn, which, core], gm_send.at[turn, which])
-            sent(sums.at[turn, which, pl.ds(0, 15)], gb_send.at[turn, which])
-            sent(sums.at[turn, which, pl.ds(0, 15)], s_send.at[turn, which])
-            sent(stage.at[turn, which, core], sm_send.at[turn, which])
+    propagate(1)
+    out_ref[0] = 0.5 * grad_users + 0.5 * scatter_end(1, USERS)
+    out_ref[1] = 0.5 * grad_items + 0.5 * scatter_end(1, ITEMS)
+    scatter_sent(1)
 
 
 def in_hbm(value):

time: 63.5 us -> 63.5 us (level)
  no operation moved by 1% of the time
where the time goes in v6:
time: 63.5 us; the launch traced here: 63.4 us
  Pallas kernels  61.4 us (97%)
  between operations  1.29 us (2%)
  local copies, waits for them, and re-layouts  0.66 us (1%)
    pallas_call x1, Pallas kernels, on_device(): pl.pallas_call(kernel, out_shape=jax.ShapeDtypeStruct((2, ROWS, WIDTH), F...  61.4 us

profile of v6, /device:TPU:1, one launch (start us, length us, event | category | flops | bytes accessed | tf_op | source)
XLA Modules:
  0.0 63.4 jit_solution(2496064352173343459)
XLA Ops:
  1.3 61.4 %propagation_layer.1 = f32[2,64,256]{2,1,0:T(8,128)S(1)} custom-call(f32[64,256]{1,0:T(8,128)} %users_hbm.1, f32[64,256]{1,0:T(8,128)} %items_hbm.1, s32[1,4]{1,0:T(1,128)} %bitcast.13, s32[1,1]{1,0:T(1,128)S(6)} %copy.10.count_hbm, s32[1,256]{1,0:T(1,128)} %bitcast.10, s32[1,256]{1,0:T(1,128)} %bitcast.11, s32[1,256]{1,0:T(1,128)} %bitcast.12, ...), custom_call_target="tpu_custom_call" | custom-call | tf_op jit(solution)/shard_map/propagation_layer/pallas_call | solution.py:422
  62.7 0.7 %slice_bitcast_fusion = (f32[64,256]{1,0:T(8,128)}, f32[64,256]{1,0:T(8,128)}) fusion(f32[2,64,256]{2,1,0:T(8,128)S(1)} %propagation_layer.1), kind=kLoop, calls=%fused_computation | loop fusion | bytes 262144 | tf_op jit(solution)/shard_map/squeeze | solution.py:488

commit v7 on v6

--- a/solution.py
+++ b/solution.py
@@ -129,15 +129,6 @@
         copy.start()
         return copy
 
-    items_load = load(0, items_hbm, items_ref)
-    users_load = load(1, users_hbm, users_ref)
-    pos_load = load(2, pos_hbm, pos_ref)
-    count_load = load(3, count_hbm, count_ref)
-    ids_load = [
-        load(4, uid_hbm, uid_ref), load(5, pid_hbm, pid_ref), load(6, nid_hbm, nid_ref)
-    ]
-    tiles_load = load(7, tiles_hbm, tiles.at[core])
-
     barrier = pltpu.get_barrier_semaphore()
     far_steps = [(other, step) for step in (2, -2) for other in (True, False)]
     near_steps = [(False, 1), (False, -1), (True, 0)]
@@ -147,6 +138,15 @@
             peers += [device(which, other, step, to_core) for to_core in range(2)]
     for peer in peers:
         pl.semaphore_signal(barrier, 1, device_id=peer, device_id_type=MESH)
+
+    items_load = load(0, items_hbm, items_ref)
+    users_load = load(1, users_hbm, users_ref)
+    pos_load = load(2, pos_hbm, pos_ref)
+    count_load = load(3, count_hbm, count_ref)
+    ids_load = [
+        load(4, uid_hbm, uid_ref), load(5, pid_hbm, pid_ref), load(6, nid_hbm, nid_ref)
+    ]
+    tiles_load = load(7, tiles_hbm, tiles.at[core])
 
     pos_load.wait()
     count_load.wait()
@@ -207,54 +207,52 @@
     def marks(cell, slot):
         return meta[cell, pl.ds(slot, 1), :]
 
-    def spread_users(turn):
-        panel = panels[turn][ITEMS]
+    def products(turn, which):
+        panel = panels[turn][1 - which]
         for cell in range(2):
             for slot in range(SLOTS):
-                rows = panel[meta_smem[cell, slot, 0] & 7].reshape(TILE, HALF)
-                prod[cell * SLOTS + slot] = jnp.dot(
-                    tiles[cell, slot], rows, preferred_element_type=F32
+                place = meta_smem[cell, slot, 0]
+                if which == USERS:
+                    rows, left = panel[place & 7], tiles[cell, slot]
+                else:
+                    rows, left = panel[(place >> 3) & 3, :, cell], tiles_t[cell, slot]
+                prod[which, cell * SLOTS + slot] = jnp.dot(
+                    left, rows.reshape(TILE, HALF), preferred_element_type=F32
                 )
 
-        def add(number, carry):
-            start = pl.ds(pl.multiple_of(lax.rem(number, 4) * ROWS, ROWS), ROWS)
+    def add_users(number):
+        start = pl.ds(pl.multiple_of(lax.rem(number, 4) * ROWS, ROWS), ROWS)
+        for cell in range(2):
+            total = jnp.zeros((ROWS, HALF), F32)
+            for slot in range(SLOTS):
+                weight = jnp.where((marks(cell, slot) >> 3) == number // 4, 1.0, 0.0)
+                total += weight.astype(F32) * prod[USERS, cell * SLOTS + slot, start, :]
+            yield cell, total
+
+    def add_items(number):
+        for owner in range(2):
+            start = (lax.rem(number, 2) * 2 + owner) * ROWS
+            start = pl.ds(pl.multiple_of(start, ROWS), ROWS)
+            total = jnp.zeros((ROWS, HALF), F32)
             for cell in range(2):
-                total = jnp.zeros((ROWS, HALF), F32)
                 for slot in range(SLOTS):
-                    weight = jnp.where((marks(cell, slot) >> 3) == number // 4, 1.0, 0.0)
-                    total += weight.astype(F32) * prod[cell * SLOTS + slot, start, :]
-                exact[USERS, number, cell] = total
-                sums[turn, USERS, number, cell] = total.astype(BF16)
+                    weight = jnp.where((marks(cell, slot) & 71) == number // 2, 1.0, 0.0)
+                    total += weight.astype(F32) * prod[ITEMS, cell * SLOTS + slot, start, :]
+            yield owner, total
+
+    def sum_blocks(turn, which, first, count):
+        def add(index, carry):
+            x = lax.rem(x_at[which] + 1 - index // count, 2)
+            along_ring = lax.rem(ring_at[which] + first + lax.rem(index, count), RING)
+            number = x * RING + along_ring
+            for part, total in (add_users if which == USERS else add_items)(number):
+                exact[which, number, part] = total
+                sums[turn, which, number, part] = total.astype(BF16)
             return carry
 
-        lax.fori_loop(0, BLOCKS, add, 0, unroll=4)
-
-    def spread_items(turn):
-        panel = panels[turn][USERS]
-        for cell in range(2):
-            for slot in range(SLOTS):
-                tile = (meta_smem[cell, slot, 0] >> 3) & 3
-                rows = panel[tile, :, cell].reshape(TILE, HALF)
-                prod[cell * SLOTS + slot] = jnp.dot(
-                    tiles_t[cell, slot], rows, preferred_element_type=F32
-                )
-
-        def add(number, carry):
-            for owner in range(2):
-                start = (lax.rem(number, 2) * 2 + owner) * ROWS
-                start = pl.ds(pl.multiple_of(start, ROWS), ROWS)
-                total = jnp.zeros((ROWS, HALF), F32)
-                for cell in range(2):
-                    for slot in range(SLOTS):
-                        weight = jnp.where((marks(cell, slot) & 71) == number // 2, 1.0, 0.0)
-                        total += weight.astype(F32) * prod[cell * SLOTS + slot, start, :]
-                exact[ITEMS, number, owner] = total
-                sums[turn, ITEMS, number, owner] = total.astype(BF16)
-            return carry
-
-        lax.fori_loop(0, BLOCKS, add, 0, unroll=4)
-
-    def scatter_start(turn, which):
+        lax.fori_loop(0, 2 * count, add, 0, unroll=count)
+
+    def scatter_far(turn, which):
         out = s_send.at[turn, which]
         for other in (True, False):
             e = int(other)
@@ -264,6 +262,9 @@
                      far.at[turn, which, e, way, 2], out, sem, along(which, 2 * step))
                 send(sums.at[turn, which, block(which, other, 3 * step)],
                      far.at[turn, which, e, way, pl.ds(0, 2)], out, sem, along(which, step))
+
+    def scatter_rest(turn, which):
+        out = s_send.at[turn, which]
         for way, step in ((0, 1), (1, -1)):
             send(sums.at[turn, which, block(which, True, step)], cross.at[turn, which, way],
                  out, sx_recv.at[turn, which], device(which, True, 0, core))
@@ -367,12 +368,14 @@
             for cell in range(2):
                 for slot in range(SLOTS):
                     tiles_t[cell, slot] = tiles[cell, slot].T
-        gather_end(turn, ITEMS)
-        spread_users(turn)
-        scatter_start(turn, USERS)
-        gather_end(turn, USERS)
-        spread_items(turn)
-        scatter_start(turn, ITEMS)
+        for which in (USERS, ITEMS):
+            gather_end(turn, 1 - which)
+            products(turn, which)
+            sum_blocks(turn, which, 3, 3)
+            scatter_far(turn, which)
+        for which in (USERS, ITEMS):
+            sum_blocks(turn, which, 6, 5)
+            scatter_rest(turn, which)
         for other in (True, False):
             for which in (USERS, ITEMS):
                 scatter_relay(turn, which, other)
@@ -445,7 +448,7 @@
             pltpu.VMEM((8, 2) + cut, BF16),
             pltpu.VMEM((8, 2) + cut, BF16),
             pltpu.VMEM((2, 2) + cut, BF16),
-            pltpu.VMEM((2 * SLOTS, TILE, HALF), F32),
+            pltpu.VMEM((2, 2 * SLOTS, TILE, HALF), F32),
             pltpu.VMEM((2, BLOCKS) + cut, F32),
             pltpu.VMEM((2, 2, BLOCKS) + cut, BF16),
             pltpu.VMEM((2, 2, 2, 2, 3, ROWS, HALF), BF16),

time: 63.5 us -> 66.7 us (1.050)
  Pallas kernels: 61.4 us -> 64.6 us
    pallas_call x1, Pallas kernels: 61.4 us -> 64.6 us  [on_device(): pl.pallas_call(kernel, out_shape=jax.ShapeDtypeStruct((2, ROWS, WIDTH), F...]
where the time goes in v7:
time: 66.7 us; the launch traced here: 66.6 us
  Pallas kernels  64.6 us (97%)
  between operations  1.29 us (2%)
    pallas_call x1, Pallas kernels, on_device(): pl.pallas_call(kernel, out_shape=jax.ShapeDtypeStruct((2, ROWS, WIDTH), F...  64.6 us

profile of v7, /device:TPU:1, one launch (start us, length us, event | category | flops | bytes accessed | tf_op | source)
XLA Modules:
  0.0 66.6 jit_solution(7441203096583960639)
XLA Ops:
  1.3 64.6 %propagation_layer.1 = f32[2,64,256]{2,1,0:T(8,128)S(1)} custom-call(f32[64,256]{1,0:T(8,128)} %users_hbm.1, f32[64,256]{1,0:T(8,128)} %items_hbm.1, s32[1,4]{1,0:T(1,128)} %bitcast.13, s32[1,1]{1,0:T(1,128)S(6)} %copy.10.count_hbm, s32[1,256]{1,0:T(1,128)} %bitcast.10, s32[1,256]{1,0:T(1,128)} %bitcast.11, s32[1,256]{1,0:T(1,128)} %bitcast.12, ...), custom_call_target="tpu_custom_call" | custom-call | tf_op jit(solution)/shard_map/propagation_layer/pallas_call | solution.py:425
  65.9 0.7 slice_bitcast_fusion

commit v8 on v6

--- a/solution.py
+++ b/solution.py
@@ -129,15 +129,6 @@
         copy.start()
         return copy
 
-    items_load = load(0, items_hbm, items_ref)
-    users_load = load(1, users_hbm, users_ref)
-    pos_load = load(2, pos_hbm, pos_ref)
-    count_load = load(3, count_hbm, count_ref)
-    ids_load = [
-        load(4, uid_hbm, uid_ref), load(5, pid_hbm, pid_ref), load(6, nid_hbm, nid_ref)
-    ]
-    tiles_load = load(7, tiles_hbm, tiles.at[core])
-
     barrier = pltpu.get_barrier_semaphore()
     far_steps = [(other, step) for step in (2, -2) for other in (True, False)]
     near_steps = [(False, 1), (False, -1), (True, 0)]
@@ -148,14 +139,14 @@
     for peer in peers:
         pl.semaphore_signal(barrier, 1, device_id=peer, device_id_type=MESH)
 
-    pos_load.wait()
-    count_load.wait()
-    filled = jnp.full((8, HALF), count_ref[0, 0], jnp.int32)
-    slot_of = lax.broadcasted_iota(jnp.int32, (8, HALF), 0)
-    placed = jnp.full((8, HALF), pos_ref[0, 0], jnp.int32)
-    for slot in range(1, SLOTS):
-        placed = jnp.where(slot_of == slot, jnp.full((8, HALF), pos_ref[0, slot], jnp.int32), placed)
-    meta[core] = jnp.where(slot_of < filled, placed, placed + 64)
+    items_load = load(0, items_hbm, items_ref)
+    users_load = load(1, users_hbm, users_ref)
+    pos_load = load(2, pos_hbm, pos_ref)
+    count_load = load(3, count_hbm, count_ref)
+    ids_load = [
+        load(4, uid_hbm, uid_ref), load(5, pid_hbm, pid_ref), load(6, nid_hbm, nid_ref)
+    ]
+    tiles_load = load(7, tiles_hbm, tiles.at[core])
 
     panels = ((user_panel_0, item_panel_0), (user_panel_1, item_panel_1))
 
@@ -383,11 +374,19 @@
 
     items_load.wait()
     own_rows(0, ITEMS, items_ref[...])
+    pl.semaphore_wait(barrier, len(peers))
+    gather_start(0, ITEMS)
     users_load.wait()
     own_rows(0, USERS, users_ref[...])
-    pl.semaphore_wait(barrier, len(peers))
-    for which in both:
-        gather_start(0, which)
+    gather_start(0, USERS)
+    pos_load.wait()
+    count_load.wait()
+    filled = jnp.full((8, HALF), count_ref[0, 0], jnp.int32)
+    slot_of = lax.broadcasted_iota(jnp.int32, (8, HALF), 0)
+    placed = jnp.full((8, HALF), pos_ref[0, 0], jnp.int32)
+    for slot in range(1, SLOTS):
+        placed = jnp.where(slot_of == slot, jnp.full((8, HALF), pos_ref[0, slot], jnp.int32), placed)
+    meta[core] = jnp.where(slot_of < filled, placed, placed + 64)
     propagate(0)
     dot = functools.partial(jnp.dot, preferred_element_type=F32)
     final_users = 0.5 * (users_ref[...] + scatter_end(0, USERS))

time: 63.5 us -> 63.9 us (level)
  no operation moved by 1% of the time
where the time goes in v8:
time: 63.9 us; the launch traced here: 63.7 us
  Pallas kernels  61.8 us (97%)
  between operations  1.29 us (2%)
  local copies, waits for them, and re-layouts  0.66 us (1%)
    pallas_call x1, Pallas kernels, on_device(): pl.pallas_call(kernel, out_shape=jax.ShapeDtypeStruct((2, ROWS, WIDTH), F...  61.8 us

profile of v8, /device:TPU:1, one launch (start us, length us, event | category | flops | bytes accessed | tf_op | source)
XLA Modules:
  0.0 63.7 jit_solution(2447891240996529856)
XLA Ops:
  1.3 61.8 %propagation_layer.1 = f32[2,64,256]{2,1,0:T(8,128)S(1)} custom-call(f32[64,256]{1,0:T(8,128)} %users_hbm.1, f32[64,256]{1,0:T(8,128)} %items_hbm.1, s32[1,4]{1,0:T(1,128)} %bitcast.13, s32[1,1]{1,0:T(1,128)S(6)} %copy.10.count_hbm, s32[1,256]{1,0:T(1,128)} %bitcast.10, s32[1,256]{1,0:T(1,128)} %bitcast.11, s32[1,256]{1,0:T(1,128)} %bitcast.12, ...), custom_call_target="tpu_custom_call" | custom-call | tf_op jit(solution)/shard_map/propagation_layer/pallas_call | solution.py:421
  63.1 0.7 %slice_bitcast_fusion = (f32[64,256]{1,0:T(8,128)}, f32[64,256]{1,0:T(8,128)}) fusion(f32[2,64,256]{2,1,0:T(8,128)S(1)} %propagation_layer.1), kind=kLoop, calls=%fused_computation | loop fusion | bytes 262144 | tf_op jit(solution)/shard_map/squeeze | solution.py:487

commit v9 on v6

--- a/solution.py
+++ b/solution.py
@@ -63,8 +63,6 @@
     exact,
     sums,
     far,
-    cross,
-    paired,
     relayed,
     last,
     load_sem,
@@ -80,7 +78,6 @@
     gb_send,
     gb_recv,
     sf_recv,
-    sx_recv,
     sl_recv,
     s_send,
     sm_send,
@@ -143,7 +140,7 @@
     near_steps = [(False, 1), (False, -1), (True, 0)]
     peers = [mate]
     for which in (USERS, ITEMS):
-        for other, step in far_steps + near_steps:
+        for other, step in far_steps + near_steps + [(True, 1), (True, -1)]:
             peers += [device(which, other, step, to_core) for to_core in range(2)]
     for peer in peers:
         pl.semaphore_signal(barrier, 1, device_id=peer, device_id_type=MESH)
@@ -265,28 +262,19 @@
                 send(sums.at[turn, which, block(which, other, 3 * step)],
                      far.at[turn, which, e, way, pl.ds(0, 2)], out, sem, along(which, step))
         for way, step in ((0, 1), (1, -1)):
-            send(sums.at[turn, which, block(which, True, step)], cross.at[turn, which, way],
-                 out, sx_recv.at[turn, which], device(which, True, 0, core))
+            for other in (True, False):
+                for to_core in range(2):
+                    send_last(turn, which, other, step, 5 * int(other) + 1 + way, to_core,
+                              sums.at[turn, which, block(which, other, step), to_core])
         for to_core in range(2):
             send_last(turn, which, True, 0, 5, to_core,
                       sums.at[turn, which, block(which, True, 0), to_core])
         send(sums.at[turn, which, block(which, False, 0), 1 - core],
-             last.at[turn, which, core * 8], sm_send.at[turn, which], sl_recv.at[turn, which], mate)
+             last.at[turn, which, core * 10], sm_send.at[turn, which], sl_recv.at[turn, which], mate)
 
     def send_last(turn, which, other, step, part, to_core, source):
-        send(source, last.at[turn, which, core * 8 + part],
+        send(source, last.at[turn, which, core * 10 + part],
              s_send.at[turn, which], sl_recv.at[turn, which], device(which, other, step, to_core))
-
-    def scatter_near(turn, which):
-        awaits(cross.at[turn, which], sx_recv.at[turn, which])
-        for way, step in ((0, 1), (1, -1)):
-            number = block(which, False, step)
-            for to_core in range(2):
-                total = exact[which, number, to_core] + cross[turn, which, way, to_core].astype(F32)
-                paired[turn, which, way, to_core] = total.astype(BF16)
-            for to_core in range(2):
-                send_last(turn, which, False, step, 1 + way, to_core,
-                          paired.at[turn, which, way, to_core])
 
     def scatter_relay(turn, which, other):
         e = int(other)
@@ -300,18 +288,18 @@
                     total += came[2].astype(F32)
                 relayed[turn, which, e, way, owner] = total.astype(BF16)
             for to_core in range(2):
-                send_last(turn, which, other, 2 * step, (6 if other else 3) + way, to_core,
+                send_last(turn, which, other, 2 * step, (8 if other else 3) + way, to_core,
                           relayed.at[turn, which, e, way, to_core])
 
     def scatter_end(turn, which):
-        awaits(last.at[turn, which, pl.ds(0, 15)], sl_recv.at[turn, which])
-        last[turn, which, core * 8] = jnp.zeros((ROWS, HALF), BF16)
+        awaits(last.at[turn, which, pl.ds(0, 19)], sl_recv.at[turn, which])
+        last[turn, which, core * 10] = jnp.zeros((ROWS, HALF), BF16)
         own = exact[which, block(which, False, 0), core]
         sides = []
         for side in range(2):
             total = jnp.where(core == side, own, 0.0)
-            for part in range(8):
-                total += last[turn, which, side * 8 + part].astype(F32)
+            for part in range(10):
+                total += last[turn, which, side * 10 + part].astype(F32)
             sides.append(total)
         return jnp.concatenate(sides, axis=1)
 
@@ -376,8 +364,6 @@
         for other in (True, False):
             for which in (USERS, ITEMS):
                 scatter_relay(turn, which, other)
-        for which in (USERS, ITEMS):
-            scatter_near(turn, which)
         if turn == 1:
             gather_sent(1)
 
@@ -449,10 +435,8 @@
             pltpu.VMEM((2, BLOCKS) + cut, F32),
             pltpu.VMEM((2, 2, BLOCKS) + cut, BF16),
             pltpu.VMEM((2, 2, 2, 2, 3, ROWS, HALF), BF16),
-            pltpu.VMEM((2, 2, 2) + cut, BF16),
-            pltpu.VMEM((2, 2, 2) + cut, BF16),
             pltpu.VMEM((2, 2, 2, 2) + cut, BF16),
-            pltpu.VMEM((2, 2, 16, ROWS, HALF), BF16),
+            pltpu.VMEM((2, 2, 20, ROWS, HALF), BF16),
             dma((8,)),
             dma,
             dma,
@@ -466,7 +450,6 @@
             dma((2, 2)),
             dma((2, 2)),
             dma((2, 2, 2, 2)),
-            dma((2, 2)),
             dma((2, 2)),
             dma((2, 2)),
             dma((2, 2)),

time: 63.5 us -> 64.2 us (1.011)
  Pallas kernels: 61.4 us -> 62.1 us
    pallas_call x1, Pallas kernels: 61.4 us -> 62.1 us  [on_device(): pl.pallas_call(kernel, out_shape=jax.ShapeDtypeStruct((2, ROWS, WIDTH), F...]
where the time goes in v9:
time: 64.2 us; the launch traced here: 64 us
  Pallas kernels  62.1 us (97%)
  between operations  1.29 us (2%)
  local copies, waits for them, and re-layouts  0.66 us (1%)
    pallas_call x1, Pallas kernels, on_device(): pl.pallas_call(kernel, out_shape=jax.ShapeDtypeStruct((2, ROWS, WIDTH), F...  62.1 us

profile of v9, /device:TPU:1, one launch (start us, length us, event | category | flops | bytes accessed | tf_op | source)
XLA Modules:
  0.0 64.0 jit_solution(14221791233627394682)
XLA Ops:
  1.3 62.1 %propagation_layer.1 = f32[2,64,256]{2,1,0:T(8,128)S(1)} custom-call(f32[64,256]{1,0:T(8,128)} %users_hbm.1, f32[64,256]{1,0:T(8,128)} %items_hbm.1, s32[1,4]{1,0:T(1,128)} %bitcast.13, s32[1,1]{1,0:T(1,128)S(6)} %copy.10.count_hbm, s32[1,256]{1,0:T(1,128)} %bitcast.10, s32[1,256]{1,0:T(1,128)} %bitcast.11, s32[1,256]{1,0:T(1,128)} %bitcast.12, ...), custom_call_target="tpu_custom_call" | custom-call | tf_op jit(solution)/shard_map/propagation_layer/pallas_call | solution.py:408
  63.4 0.7 %slice_bitcast_fusion = (f32[64,256]{1,0:T(8,128)}, f32[64,256]{1,0:T(8,128)}) fusion(f32[2,64,256]{2,1,0:T(8,128)S(1)} %propagation_layer.1), kind=kLoop, calls=%fused_computation | loop fusion | bytes 262144 | tf_op jit(solution)/shard_map/squeeze | solution.py:471
